TPU v7x, 128 devices: a whole 4x4x4 slice. The times are simulated.
128 devices in a mesh: seq: 16 (over x_hi, z, core), fsdp: 8 (over x_lo, y).
Axes of the slice: x: 4 (x_hi: 2, x_lo: 2; x = x_hi * 2 + x_lo), y: 4, z: 4, core: 2. Of those that a mesh axis runs over, the one named last changes fastest.
Arguments:
- tokens: bfloat16 [8, 2048, 1024], P('fsdp', 'seq'), may hold values from -6 to 6
- out_grad: bfloat16 [8, 2048, 1024], P('fsdp', 'seq'), may hold values from -6 to 6
- w_query: bfloat16 [1024, 2048], P('fsdp'), may hold values from -0.1875 to 0.1875
- w_key: bfloat16 [1024, 1024], P('fsdp'), may hold values from -0.1875 to 0.1875
- w_value: bfloat16 [1024, 1024], P('fsdp'), may hold values from -0.1875 to 0.1875
- w_out: bfloat16 [2048, 1024], P('fsdp'), may hold values from -0.125 to 0.125
- w_gate: bfloat16 [1024, 3072], P('fsdp'), may hold values from -0.1875 to 0.1875
- w_up: bfloat16 [1024, 3072], P('fsdp'), may hold values from -0.1875 to 0.1875
- w_down: bfloat16 [3072, 1024], P('fsdp'), may hold values from -0.109375 to 0.109375
- gain_query: float32 [2048], replicated, may hold values from 0.25 to 1.75
- gain_key: float32 [1024], replicated, may hold values from 0.25 to 1.75
- gain_attn: float32 [1024], replicated, may hold values from 0.25 to 1.75
- gain_mlp: float32 [1024], replicated, may hold values from 0.25 to 1.75
Outputs:
- output: bfloat16 [8, 2048, 1024], P('fsdp', 'seq')
- input_grad: bfloat16 [8, 2048, 1024], P('fsdp', 'seq')
- grad_query: float32 [1024, 2048], P(('seq', 'fsdp'))
- grad_key: float32 [1024, 1024], P(('seq', 'fsdp'))
- grad_value: float32 [1024, 1024], P(('seq', 'fsdp'))
- grad_out: float32 [2048, 1024], P(('seq', 'fsdp'))
- grad_gate: float32 [1024, 3072], P(('seq', 'fsdp'))
- grad_up: float32 [1024, 3072], P(('seq', 'fsdp'))
- grad_down: float32 [3072, 1024], P(('seq', 'fsdp'))
- grad_gain_query: float32 [2048], P(('seq', 'fsdp'))
- grad_gain_key: float32 [1024], P(('seq', 'fsdp'))
- grad_gain_attn: float32 [1024], P(('seq', 'fsdp'))
- grad_gain_mlp: float32 [1024], P(('seq', 'fsdp'))
All inputs are finite; a program needn't handle non-finite values.
Results may differ from a plain program's by a relative error of at most 0.039.
Values may be sent and summed in bfloat16 or wider, within the bound.
No kernel may reach another device: no remote copies, remote signals or barrier semaphores. Data moves between devices by JAX's collectives and lax.ppermute only.
A program may use at most 192 MiB of HBM per device.

v0:
```python
import functools
import math

import jax
import jax.numpy as jnp
from jax import lax
from jax.experimental import pallas as pl
from jax.experimental.pallas import tpu as pltpu
from jax.sharding import PartitionSpec as P

BF16 = jnp.bfloat16
F32 = jnp.float32
DH = 128
EPS = 1e-06
THETA = 1000000.0
MASKED = -1e30
LOG2E = math.log2(math.e)
QUERY_SCALE = DH ** (-0.5) * LOG2E
VMEM_BYTES = 20 * 1024 * 1024
VMEM = pl.BlockSpec(memory_space=pltpu.VMEM)
SMEM = pl.BlockSpec(memory_space=pltpu.SMEM)
ANY = pl.BlockSpec(memory_space=pl.ANY)
SMALL = 64 * 1024
NT = (((1,), (1,)), ((), ()))

SEQ_PLACES = [(xh, z, c) for xh in range(2) for z in range(4) for c in range(2)]


def seq_index(xh, z, c):
    return xh * 8 + (z % 4) * 2 + c


CORE_SWAP = [(i, i ^ 1) for i in range(16)]
LOW_TO_HIGH = [(i, i + 8) for i in range(8)]
HIGH_TO_LOW = [(i + 8, i) for i in range(8)]
X_SWAP = [(i, i ^ 8) for i in range(16)]


def from_z(k):
    return [(seq_index(xh, z + k, c), seq_index(xh, z, c)) for xh, z, c in SEQ_PLACES]


def to_z(k):
    return [(seq_index(xh, z, c), seq_index(xh, z + k, c)) for xh, z, c in SEQ_PLACES]


def across(pairs):
    return [(seq * 8 + f, to_seq * 8 + to_f) for seq, f, to_seq, to_f in pairs]


TURN = across(
    (xh * 8 + a, f, xh * 8 + f, a) for xh in range(2) for a in range(8) for f in range(8)
)
Z_SWAP = [(i, i ^ 2) for i in range(16)]
FAR_SWAP = [(i, i ^ 4) for i in range(16)]
OUT_HOME = [(xh * 8 + a, 2 * a + xh) for xh in range(2) for a in range(8)]
DOWN_HOME = across(
    (seq_index(xh, 2 * zh + zl, c), f, 2 * f + zl, 4 * c + 2 * xh + zh)
    for xh in range(2) for zh in range(2) for zl in range(2) for c in range(2) for f in range(8)
)


def swap(value, pairs):
    return lax.ppermute(value, "seq", pairs)


def after(value, *others):
    return lax.optimization_barrier((value, *others))[0]


def gather_group(block):
    far = {k: swap(block, from_z(k)) for k in (2, 1, 3)}
    mine = [block, far[1], far[2], far[3]]
    return mine + [swap(v, CORE_SWAP) for v in mine]


def scatter_group(mine, part):
    rows = [slice(k * 128, k * 128 + 128) for k in range(4)]
    out = None
    for k in (2, 1, 3, 0):
        piece = mine[rows[k]] + swap(part[rows[k]], CORE_SWAP).astype(F32)
        if k:
            piece = swap(piece.astype(BF16), to_z(k)).astype(F32)
        out = piece if out is None else out + piece
    return out


def gather_pair(block):
    mine = [block, swap(block, Z_SWAP)]
    return mine + [swap(v, CORE_SWAP) for v in mine]


def scatter_pair(mine, part, later=()):
    far = mine[128:] + swap(part[128:], CORE_SWAP).astype(F32)
    far, *later = lax.optimization_barrier((far.astype(BF16), *later))
    far = swap(far, Z_SWAP).astype(F32)
    return mine[:128] + swap(part[:128], CORE_SWAP).astype(F32) + far, later


def sum_group(rows):
    groups = rows.shape[0] // 8
    other = swap(rows, CORE_SWAP).reshape(groups, 2, 4, 128)
    pair = rows.reshape(groups, 2, 4, 128) + jnp.concatenate([other[:, 1:], other[:, :1]], axis=1)
    odd = lax.axis_index("seq") // 2 % 2 == 1
    got = swap(pair, Z_SWAP)
    up = jnp.concatenate([got[:, :, 3:], got[:, :, :3]], axis=2)
    down = jnp.concatenate([got[:, :, 1:], got[:, :, :1]], axis=2)
    pair = pair + jnp.where(odd, down, up)
    got = swap(pair, FAR_SWAP)
    pair = pair + jnp.concatenate([got[:, :, 2:], got[:, :, :2]], axis=2)
    return pair.reshape(rows.shape)


def column(row):
    return jnp.transpose(jnp.broadcast_to(row, (128, 128)))


def row_sums(values):
    return jnp.sum(jnp.transpose(values), axis=0, keepdims=True)


def shaped(shape, dtype):
    return jax.ShapeDtypeStruct(shape, dtype)


class Kept:
    def __init__(self, value):
        self.value = value


def in_hbm(*values):
    return [Kept(v) for v in values]


def kernel_call(body, outs, inputs, scratch=(), flops=0, nbytes=0):
    hbm_outs = [isinstance(o, Kept) for o in outs]
    hbm_ins = [isinstance(x, Kept) for x in inputs]
    outs = [o.value if isinstance(o, Kept) else o for o in outs]
    inputs = [x.value if isinstance(x, Kept) else x for x in inputs]
    groups = [x if isinstance(x, list) else [x] for x in inputs]
    flat = [a for group in groups for a in group]
    joined = [
        shaped((sum(a.shape[0] for a in group),) + group[0].shape[1:], group[0].dtype)
        for group in groups
    ]

    def large(s):
        return math.prod(s.shape) * s.dtype.itemsize >= SMALL

    def where(s):
        return ANY if large(s) else SMEM if s.dtype == jnp.int32 else VMEM

    out_shapes = [joined[o] if isinstance(o, int) else o for o in outs]
    in_buffers = [pltpu.VMEM(s.shape, s.dtype) for s in joined if large(s)]
    out_buffers = [
        pltpu.VMEM(o.shape, o.dtype) for o in outs if not isinstance(o, int) and large(o)
    ]

    def whole(*refs):
        refs = list(refs)

        def pull(count):
            taken = refs[:count]
            del refs[:count]
            return taken

        in_refs, out_refs = pull(len(flat)), pull(len(outs))
        in_space, out_space = pull(len(in_buffers)), pull(len(out_buffers))
        own, (in_sem, out_sem) = pull(len(scratch)), refs
        loads, ins, at = {}, [], 0
        for group, s in zip(groups, joined):
            if not large(s):
                ins.append(in_refs[at])
                at += 1
                continue
            space, row = in_space.pop(0), 0
            loads[id(space)] = []
            for a in group:
                copy = pltpu.make_async_copy(
                    in_refs[at], space.at[pl.ds(row, a.shape[0])], in_sem.at[at]
                )
                copy.start()
                loads[id(space)].append(copy)
                row, at = row + a.shape[0], at + 1
            ins.append(space)
        made, stores = [], {}
        for k, (o, s, ref) in enumerate(zip(outs, out_shapes, out_refs)):
            if not large(s):
                made.append(ref)
                continue
            space = ins[o] if isinstance(o, int) else out_space.pop(0)
            stores[id(space)] = pltpu.make_async_copy(space, ref, out_sem.at[k])
            if not isinstance(o, int):
                made.append(space)
        started = []

        def ready(*spaces):
            for space in spaces:
                for copy in loads.pop(id(space), ()):
                    copy.wait()

        def done(*spaces):
            for space in spaces:
                copy = stores.pop(id(space))
                copy.start()
                started.append(copy)

        body(ready, done, *ins, *made, *own)
        for key in list(stores):
            copy = stores.pop(key)
            copy.start()
            started.append(copy)
        for copy in started:
            copy.wait()

    shapes = [pltpu.HBM(s.shape, s.dtype) if hbm else s for s, hbm in zip(out_shapes, hbm_outs)]
    return pl.pallas_call(
        whole,
        out_shape=tuple(shapes),
        in_specs=[where(s) for group, s in zip(groups, joined) for _ in group],
        out_specs=tuple(where(s) for s in out_shapes),
        scratch_shapes=[
            *in_buffers, *out_buffers, *scratch,
            pltpu.SemaphoreType.DMA((len(flat),)), pltpu.SemaphoreType.DMA((len(outs),)),
        ],
        compiler_params=pltpu.CompilerParams(vmem_limit_bytes=VMEM_BYTES),
        cost_estimate=pl.CostEstimate(flops=flops, bytes_accessed=nbytes, transcendentals=0),
    )(
        *[
            pltpu.with_memory_space_constraint(a, pltpu.HBM) if hbm else a
            for group, hbm in zip(groups, hbm_ins)
            for a in group
        ],
    )


def root(total, width):
    return lax.rsqrt(total * (1.0 / width) + EPS)


def project_body(
    ready, done, x_all, weight, gain_q, gain_k, cos, sin,
    q_raw, k_raw, q_rot, kv_rot, squares,
):
    ready(x_all, weight, cos, sin)
    done(x_all)

    def step(t, carry):
        at = pl.multiple_of(t * 256, 256)
        made = jnp.dot(x_all[pl.ds(at, 256), :], weight[...], preferred_element_type=F32)
        for part in range(2):
            rows = pl.ds(at + part * 128, 128)
            block = t * 2 + part
            here = made[part * 128 : part * 128 + 128]
            q, k = here[:, :256], here[:, 256:384]
            kv_rot[rows, 128:] = here[:, 384:].astype(BF16)
            q_raw[rows, :] = q
            k_raw[rows, :] = k
            squares[pl.ds(block, 1), :] = row_sums(
                q[:, :128] * q[:, :128] + q[:, 128:] * q[:, 128:]
            )
            squares[pl.ds(block + 8, 1), :] = row_sums(k * k)
            cosine, sine = cos[rows, :], sin[rows, :]
            for head in range(2):
                lanes = slice(head * 128, head * 128 + 128)
                turn = q[:, lanes] * gain_q[:, lanes]
                q_rot[rows, lanes] = (turn * cosine + pltpu.roll(turn, 64, 1) * sine).astype(BF16)
            turn = k * gain_k[...]
            kv_rot[rows, :128] = (turn * cosine + pltpu.roll(turn, 64, 1) * sine).astype(BF16)
        return carry

    lax.fori_loop(0, 4, step, 0)


def spot(place, block):
    z = lax.rem(place[1] + block % 4, 4)
    c = place[2] if block < 4 else 1 - place[2]
    return z, c


def attend_body(
    ready, done, place, q_rot, kv_rot, kv_low, squares, squares_low,
    out_raw, out_low, out_turned, q_tiles, keys, vals, logs, vals_t,
):
    ready(q_rot, kv_rot, kv_low)
    for b in range(8):
        rows = slice(b * 128, b * 128 + 128)
        z, c = spot(place, b)
        r = column(root(squares[b : b + 1, :], 2048.0)) * QUERY_SCALE
        inner = pl.ds(pl.multiple_of(c * 128, 128), 128)
        for head in range(2):
            q = q_rot[rows, head * 128 : head * 128 + 128].astype(F32)
            q_tiles[z * 2 + head, inner, :] = (q * r).astype(BF16)
        at = pl.ds(pl.multiple_of(1024 + z * 256 + c * 128, 128), 128)
        r = column(root(squares[8 + b : 9 + b, :], 1024.0))
        keys[at, :] = (kv_rot[rows, :128].astype(F32) * r).astype(BF16)
        vals[at, :] = kv_rot[rows, 128:]
        r = column(root(squares_low[b : b + 1, :], 1024.0))
        keys[rows, :] = (kv_low[rows, :128].astype(F32) * r).astype(BF16)
        vals[rows, :] = kv_low[rows, 128:]
    done(q_tiles, keys, vals)
    vals_t[...] = jnp.transpose(vals[...].astype(F32)).astype(BF16)
    allowed = lax.broadcasted_iota(jnp.int32, (256, 256), 0) <= lax.broadcasted_iota(
        jnp.int32, (256, 256), 1
    )

    def queries(first, i):
        at_diagonal = 1024 + i * 256
        ranges = [(first, at_diagonal)] if at_diagonal > first else []
        for head in range(2):
            q = q_tiles[i * 2 + head]
            scores = [
                lax.dot_general(keys[lo:hi, :], q, NT, preferred_element_type=F32)
                for lo, hi in ranges + [(at_diagonal, at_diagonal + 256)]
            ]
            scores[-1] = jnp.where(allowed, scores[-1], MASKED)
            tops = [jnp.max(s, axis=0, keepdims=True) for s in scores]
            top = functools.reduce(jnp.maximum, tops)
            total, acc = 0.0, 0.0
            for s, (lo, hi) in zip(scores, ranges + [(at_diagonal, at_diagonal + 256)]):
                p = jnp.exp2(s - top)
                total = total + jnp.sum(p, axis=0, keepdims=True)
                acc = acc + jnp.dot(
                    vals_t[:, lo:hi], p.astype(BF16), preferred_element_type=F32
                )
            turned = acc / total
            out = jnp.transpose(turned)
            turned = turned.astype(BF16)
            logs[i * 2 + head : i * 2 + head + 1, :] = top + jnp.log2(total)
            for c in range(2):
                block = lax.rem(i - place[1] + 4, 4) + 4 * jnp.abs(c - place[2])
                at = pl.ds(pl.multiple_of(block * 128, 128), 128)
                lanes = slice(head * 128, head * 128 + 128)
                out_raw[at, lanes] = out[c * 128 : c * 128 + 128, :]
                out_low[at, lanes] = out[c * 128 : c * 128 + 128, :].astype(BF16)
                out_turned[lanes, at] = turned[:, c * 128 : c * 128 + 128]

    @pl.when(place[0] == 1)
    def _():
        for i in range(4):
            queries(0, i)

    @pl.when(place[0] == 0)
    def _():
        for i in range(4):
            queries(1024, i)

    done(out_raw, out_low, out_turned)


def output_body(ready, done, mixed, w_out, a_mine, a_part):
    ready(mixed, w_out)

    def project(t, carry):
        at = pl.ds(pl.multiple_of(t * 256, 256), 256)
        far = pl.ds(pl.multiple_of(512 + t * 256, 256), 256)
        a_part[at, :] = jnp.dot(mixed[far, :], w_out[...], preferred_element_type=F32).astype(BF16)
        a_mine[at, :] = jnp.dot(mixed[at, :], w_out[...], preferred_element_type=F32)
        return carry

    lax.fori_loop(0, 2, project, 0)


def output_back_body(
    ready, done, place, out_raw, w_out, da_all, mixed_turned, d_tiles, deltas, grad_out
):
    ready(out_raw, w_out, da_all)
    for b in range(8):
        rows = slice(b * 128, b * 128 + 128)
        z, c = spot(place, b)
        inner = pl.ds(pl.multiple_of(c * 128, 128), 128)
        d_out = lax.dot_general(
            da_all[rows, :], w_out[...], NT, preferred_element_type=F32
        ).astype(BF16)
        for head in range(2):
            lanes = slice(head * 128, head * 128 + 128)
            grad = d_out[:, lanes]
            d_tiles[z * 2 + head, inner, :] = grad
            deltas[z * 2 + head, pl.ds(c, 1), :] = row_sums(grad.astype(F32) * out_raw[rows, lanes])
    done(d_tiles)
    ready(mixed_turned)
    for m in range(4):
        lanes = slice(m * 256, m * 256 + 256)
        made = jnp.dot(mixed_turned[...], da_all[:, lanes], preferred_element_type=F32).astype(BF16)
        for j in range(2):
            for f in range(8):
                to, at = f * 32 + j * 16, j * 128 + f * 16
                grad_out[to : to + 16, lanes] = made[at : at + 16]


def attend_back_body(
    ready, done, place, q_tiles, keys, vals, logs, d_tiles, deltas,
    dq, dk, dv, d_low, dots, keys_t, dk_acc, dv_acc,
):
    ready(keys)
    keys_t[...] = jnp.transpose(keys[...].astype(F32)).astype(BF16)
    ready(q_tiles, vals, d_tiles)
    dk_acc[...] = jnp.zeros_like(dk_acc)
    dv_acc[...] = jnp.zeros_like(dv_acc)
    allowed = lax.broadcasted_iota(jnp.int32, (256, 256), 0) <= lax.broadcasted_iota(
        jnp.int32, (256, 256), 1
    )

    def queries(first, i):
        at_diagonal = 1024 + i * 256
        q = [q_tiles[i * 2 + head] for head in range(2)]
        grad = [d_tiles[i * 2 + head] for head in range(2)]
        log = [logs[i * 2 + head : i * 2 + head + 1, :] for head in range(2)]
        delta = [
            jnp.concatenate([deltas[i * 2 + head, 0:1, :], deltas[i * 2 + head, 1:2, :]], axis=1)
            for head in range(2)
        ]
        total = [0.0, 0.0]
        for lo in range(first, at_diagonal + 256, 256):
            at = slice(lo, lo + 256)
            k, v = keys[at, :], vals[at, :]
            dk_tile, dv_tile = dk_acc[at, :], dv_acc[at, :]
            for head in range(2):
                s = lax.dot_general(k, q[head], NT, preferred_element_type=F32)
                p = jnp.exp2(s - log[head])
                if lo == at_diagonal:
                    p = jnp.where(allowed, p, 0.0)
                dp = lax.dot_general(v, grad[head], NT, preferred_element_type=F32)
                ds = (p * (dp - delta[head])).astype(BF16)
                dv_tile += jnp.dot(p.astype(BF16), grad[head], preferred_element_type=F32)
                dk_tile += jnp.dot(ds, q[head], preferred_element_type=F32)
                total[head] = total[head] + jnp.dot(
                    keys_t[:, at], ds, preferred_element_type=F32
                )
            dk_acc[at, :] = dk_tile
            dv_acc[at, :] = dv_tile
        dot = jnp.zeros((1, 256), F32)
        for head in range(2):
            out = jnp.transpose(total[head]) * DH ** (-0.5)
            dot += jnp.sum(total[head] * jnp.transpose(q[head].astype(F32)), axis=0, keepdims=True)
            for c in range(2):
                block = lax.rem(i - place[1] + 4, 4) + 4 * jnp.abs(c - place[2])
                at = pl.ds(pl.multiple_of(block * 128, 128), 128)
                dq[at, head * 128 : head * 128 + 128] = out[c * 128 : c * 128 + 128, :].astype(BF16)
        for c in range(2):
            block = lax.rem(i - place[1] + 4, 4) + 4 * jnp.abs(c - place[2])
            dots[pl.ds(block, 1), :] = dot[:, c * 128 : c * 128 + 128] * (1.0 / LOG2E)

    @pl.when(place[0] == 1)
    def _():
        for i in range(4):
            queries(0, i)

    @pl.when(place[0] == 0)
    def _():
        for i in range(4):
            queries(1024, i)

    for b in range(8):
        rows = slice(b * 128, b * 128 + 128)
        z, c = spot(place, b)
        at = pl.ds(pl.multiple_of(1024 + z * 256 + c * 128, 128), 128)
        key_grad = dk_acc[at, :] * (1.0 / LOG2E)
        dk[rows, :] = key_grad
        dv[rows, :] = dv_acc[at, :]
        dots[8 + b : 9 + b, :] = row_sums(key_grad * keys[at, :].astype(F32))
        key_grad = dk_acc[rows, :] * (1.0 / LOG2E)
        d_low[rows, :128] = key_grad.astype(BF16)
        d_low[rows, 128:] = dv_acc[rows, :].astype(BF16)
        dots[16 + b : 17 + b, :] = row_sums(key_grad * keys[rows, :].astype(F32))


def unproject_body(
    ready, done, place, dq, dk, dv, d_got, q_raw, k_raw, squares, dots, dots_got, cos, sin,
    gain_q, gain_k, x_turned, gains, d_made, sent, sums,
):
    sums[...] = jnp.zeros_like(sums)
    ready(dq, dk, dv, d_got, q_raw, k_raw, cos, sin)

    def step(b, carry):
        rows = pl.ds(pl.multiple_of(b * 128, 128), 128)
        cosine, sine = cos[rows, :], sin[rows, :]
        r = column(root(squares[pl.ds(b, 1), :], 2048.0))
        mean = column(dots[pl.ds(b, 1), :]) * (1.0 / 2048.0)
        for head in range(2):
            lanes = slice(head * 128, head * 128 + 128)
            turn = dq[rows, lanes].astype(F32)
            d_norm = turn * cosine - pltpu.roll(turn, 64, 1) * sine
            hat = q_raw[rows, lanes] * r
            sums[0:1, lanes] += jnp.sum(d_norm * hat, axis=0, keepdims=True)
            d_made[rows, lanes] = (r * (d_norm * gain_q[:, lanes] - hat * mean)).astype(BF16)
        r = column(root(squares[pl.ds(b + 8, 1), :], 1024.0))
        mean = column(dots[pl.ds(b + 8, 1), :] + dots_got[pl.ds(b, 1), :]) * (1.0 / 1024.0)
        turn = dk[rows, :] + d_got[rows, :128].astype(F32)
        d_norm = turn * cosine - pltpu.roll(turn, 64, 1) * sine
        hat = k_raw[rows, :] * r
        sums[0:1, 256:] += jnp.sum(d_norm * hat, axis=0, keepdims=True)
        d_made[rows, 256:384] = (r * (d_norm * gain_k[...] - hat * mean)).astype(BF16)
        d_made[rows, 384:] = (dv[rows, :] + d_got[rows, 128:].astype(F32)).astype(BF16)
        return carry

    lax.fori_loop(0, 8, step, 0)
    done(d_made)
    ready(x_turned, gains)

    def grad(t, carry):
        rows = pl.ds(pl.multiple_of(t * 256, 256), 256)
        sent[rows, :512] = jnp.dot(
            x_turned[rows, :], d_made[...], preferred_element_type=F32
        ).astype(BF16)
        sent[rows, 512:] = gains[rows, :]
        return carry

    lax.fori_loop(0, 4, grad, 0)
    extra = 0.0
    for lo, width, each, first in ((0, 256, 16, 0), (256, 128, 8, 16)):
        row = lax.broadcasted_iota(jnp.int32, (128, width), 0) // 8
        lane = lax.broadcasted_iota(jnp.int32, (128, width), 1) // each
        spread = jnp.where(row == lane, sums[0:1, lo : lo + width], 0.0).astype(BF16)
        lane = lax.broadcasted_iota(jnp.int32, (width, 128), 0) % each + first
        pick = jnp.where(lane == lax.broadcasted_iota(jnp.int32, (width, 128), 1), 1.0, 0.0)
        extra = extra + jnp.dot(spread, pick.astype(BF16), preferred_element_type=F32)
    rows = pl.ds(pl.multiple_of((place[1] * 2 + place[2]) * 128, 128), 128)
    sent[rows, 512:] = (gains[rows, :].astype(F32) + extra).astype(BF16)


def input_body(ready, done, d_made, weight, dx_mine, dx_part):
    ready(d_made, weight)

    def step(t, carry):
        at = pl.ds(pl.multiple_of(t * 256, 256), 256)
        far = pl.ds(pl.multiple_of(512 + t * 256, 256), 256)
        dx_part[at, :] = lax.dot_general(
            d_made[far, :], weight[...], NT, preferred_element_type=F32
        ).astype(BF16)
        dx_mine[at, :] = lax.dot_general(
            d_made[at, :], weight[...], NT, preferred_element_type=F32
        )
        return carry

    lax.fori_loop(0, 2, step, 0)


def expand_body(ready, done, h_all, weight, gate, up, expanded, m_mine, m_part, down):
    ready(weight)
    for f in range(8):
        down[f * 96 : f * 96 + 96, :768] = weight[f * 128 : f * 128 + 96, 1536:]
        for m in range(3):
            down[f * 96 + m * 32 : f * 96 + m * 32 + 32, 768:] = weight[
                f * 128 + 96 : f * 128 + 128, 1536 + m * 256 : 1792 + m * 256
            ]

    done(down)
    ready(h_all)
    done(h_all)

    def widen(n, carry):
        lanes = pl.ds(pl.multiple_of(n * 256, 256), 256)
        upper = pl.ds(pl.multiple_of(768 + n * 256, 256), 256)
        g = jnp.dot(h_all[...], weight[:, lanes], preferred_element_type=F32)
        u = jnp.dot(h_all[...], weight[:, upper], preferred_element_type=F32)
        gate[:, lanes] = g
        up[:, lanes] = u
        expanded[:, lanes] = (g * jax.nn.sigmoid(g) * u).astype(BF16)
        return carry

    lax.fori_loop(0, 3, widen, 0)
    done(gate, up, expanded)

    def narrow(n, carry):
        lanes = pl.ds(pl.multiple_of(n * 256, 256), 256)
        m = jnp.dot(expanded[...], down[:, lanes], preferred_element_type=F32)
        m_mine[:, lanes] = m[:256]
        m_part[:, lanes] = m[256:].astype(BF16)
        return carry

    lax.fori_loop(0, 4, narrow, 0)


def expand_back_body(ready, done, dm_all, gate, up, weight, down, d_gu, dh_mine, dh_part):
    ready(dm_all, gate, up, down)
    done(dm_all)

    def widen(n, carry):
        lanes = pl.ds(pl.multiple_of(n * 256, 256), 256)
        upper = pl.ds(pl.multiple_of(768 + n * 256, 256), 256)
        de = lax.dot_general(dm_all[...], down[lanes, :], NT, preferred_element_type=F32)
        g = gate[:, lanes]
        sig = jax.nn.sigmoid(g)
        d_gu[:, lanes] = (de * up[:, lanes] * sig * (1.0 + g * (1.0 - sig))).astype(BF16)
        d_gu[:, upper] = (de * (g * sig)).astype(BF16)
        return carry

    lax.fori_loop(0, 3, widen, 0)
    done(d_gu)
    ready(weight)

    def narrow(n, carry):
        lanes = pl.ds(pl.multiple_of(n * 256, 256), 256)
        dh = lax.dot_general(d_gu[...], weight[lanes, :1536], NT, preferred_element_type=F32)
        dh_mine[:, lanes] = dh[:256]
        dh_part[:, lanes] = dh[256:].astype(BF16)
        return carry

    lax.fori_loop(0, 4, narrow, 0)


def expand_grad_body(ready, done, h_turned, d_gu, expanded, dm_all, out, expanded_t):
    ready(expanded)
    expanded_t[...] = jnp.transpose(expanded[...].astype(F32)).astype(BF16)

    ready(h_turned, d_gu, dm_all)

    def widen(n, carry):
        lanes = pl.ds(pl.multiple_of(n * 256, 256), 256)
        out[:, lanes] = jnp.dot(
            h_turned[...], d_gu[:, lanes], preferred_element_type=F32
        ).astype(BF16)
        return carry

    lax.fori_loop(0, 6, widen, 0)
    for n in range(4):
        made = jnp.dot(
            expanded_t[...], dm_all[:, n * 256 : n * 256 + 256], preferred_element_type=F32
        ).astype(BF16)
        for f in range(16):
            if n < 3:
                out[f * 64 : f * 64 + 48, 1536 + n * 256 : 1792 + n * 256] = made[
                    f * 48 : f * 48 + 48
                ]
                continue
            for m in range(3):
                out[f * 64 + 48 : f * 64 + 64, 1536 + m * 256 : 1792 + m * 256] = made[
                    f * 48 + m * 16 : f * 48 + m * 16 + 16
                ]


def norm_scale(values):
    return lax.rsqrt(jnp.mean(values * values, axis=-1, keepdims=True) + EPS)


def norm_back(upstream, normed, scaling):
    return scaling * (upstream - normed * jnp.mean(upstream * normed, axis=-1, keepdims=True))


def rotary_tables(first, z, c):
    half = DH // 2
    k = jnp.arange(4, dtype=jnp.int32)
    starts = jnp.concatenate([((z + k) % 4) * 256 + c * 128, ((z + k) % 4) * 256 + (1 - c) * 128])
    places = (first + starts[:, None] + jnp.arange(128, dtype=jnp.int32)[None, :]).reshape(1024)
    inverse = THETA ** (-(jnp.arange(half, dtype=F32) * (2.0 / DH)))
    angles = places.astype(F32)[:, None] * inverse[None, :]
    cosine, sine = jnp.cos(angles), jnp.sin(angles)
    return (
        jnp.concatenate([cosine, cosine], axis=-1),
        jnp.concatenate([-sine, sine], axis=-1),
    )


def dot(a, b):
    return jnp.dot(a, b, preferred_element_type=F32)


def dot_nt(a, b):
    return lax.dot_general(a, b, NT, preferred_element_type=F32)


def dot_tn(a, b):
    return lax.dot_general(a, b, (((0,), (0,)), ((), ())), preferred_element_type=F32)


def on_device(
    tokens, out_grad, w_query, w_key, w_value, w_out, w_gate, w_up, w_down,
    gain_query, gain_key, gain_attn, gain_mlp,
):
    seq = lax.axis_index("seq")
    xh, zc = seq // 8, seq % 8
    z, c = zc // 2, zc % 2
    quarter = (z % 2) * 2 + c
    place = jnp.stack([xh, z, c]).astype(jnp.int32)
    inputs = tokens[0]

    def columns(weight, width):
        return lax.dynamic_slice_in_dim(weight, zc * width, width, 1)

    def spread(block):
        return lax.all_to_all(
            jnp.broadcast_to(block[None], (8,) + block.shape),
            "fsdp", split_axis=0, concat_axis=0, tiled=True,
        ).reshape(8 * block.shape[0], block.shape[1])

    x_blocks = gather_group(inputs)
    weight = spread(
        jnp.concatenate(
            [columns(w_query, 256), columns(w_key, 128), columns(w_value, 128)], axis=1
        )
    )
    w_out_rows = lax.ppermute(
        after(lax.dynamic_slice_in_dim(w_out, zc * 32, 32, 0), *x_blocks[1:4]),
        ("seq", "fsdp"),
        TURN,
    )

    def quarters(weight):
        part = lax.dynamic_slice_in_dim(weight.reshape(128, 8, 384), quarter * 96, 96, 2)
        return part.reshape(128, 768)

    down = lax.dynamic_slice_in_dim(w_down, quarter * 96, 96, 0)
    packed = jnp.concatenate(
        [
            down[:, :768],
            jnp.concatenate([down[m * 32 : m * 32 + 32, 768:] for m in range(3)], axis=1),
        ],
        axis=0,
    )
    w_mlp = jnp.concatenate([quarters(w_gate), quarters(w_up), packed], axis=1)
    weight, w_mlp, w_out_rows = lax.optimization_barrier((weight, w_mlp, w_out_rows))

    cosine, sine = rotary_tables(xh * 1024, z, c)
    gain_q = lax.dynamic_slice_in_dim(gain_query, zc * 256, 256, 0)[None]
    gain_k = lax.dynamic_slice_in_dim(gain_key, zc * 128, 128, 0)[None]
    x_all, q_raw, k_raw, q_rot, kv_rot, squares = kernel_call(
        project_body,
        [
            *in_hbm(
                0, shaped((1024, 256), F32), shaped((1024, 128), F32),
                shaped((1024, 256), BF16), shaped((1024, 256), BF16),
            ),
            shaped((16, 128), F32),
        ],
        [x_blocks, weight, gain_q, gain_k, cosine, sine],
        flops=2 * 1024 * 1024 * 512, nbytes=9 << 20,
    )

    kv_low = swap(kv_rot, LOW_TO_HIGH)
    w_mlp = lax.all_gather(after(w_mlp, squares), "fsdp", axis=0, tiled=True)
    squares = sum_group(squares)
    squares_low = swap(squares[8:], LOW_TO_HIGH)
    w_out_rows = spread(after(w_out_rows, squares_low))
    out_raw, mixed, mixed_turned, q_tiles, keys, vals, logs = kernel_call(
        attend_body,
        [
            *in_hbm(
                shaped((1024, 256), F32), shaped((1024, 256), BF16), shaped((256, 1024), BF16),
                shaped((8, 256, 128), BF16), shaped((2048, 128), BF16), shaped((2048, 128), BF16),
            ),
            shaped((8, 256), F32),
        ],
        [place, *in_hbm(q_rot, kv_rot), kv_low, squares, squares_low],
        [pltpu.VMEM((128, 2048), BF16)],
        flops=4 * 1024 * 2048 * 256, nbytes=9 << 20,
    )
    a_mine, a_part = kernel_call(
        output_body,
        [shaped((512, 1024), F32), shaped((512, 1024), BF16)],
        [*in_hbm(mixed), w_out_rows],
        flops=2 * 1024 * 1024 * 256, nbytes=5 << 20,
    )
    x_turned = x_all.T

    attended = scatter_group(a_mine, a_part)
    attended, x_turned = lax.optimization_barrier((attended, x_turned))
    attn_scale = norm_scale(attended)
    attn_hat = attended * attn_scale
    hidden_state = inputs.astype(F32) + attn_hat * gain_attn
    h_all, gate, up, expanded, m_mine, m_part, w_down_rows = kernel_call(
        expand_body,
        [
            0, shaped((512, 768), F32), shaped((512, 768), F32), shaped((512, 768), BF16),
            shaped((256, 1024), F32), shaped((256, 1024), BF16), shaped((768, 1024), BF16),
        ],
        [
            gather_pair(hidden_state.astype(BF16)), *in_hbm(w_mlp),
        ],
        flops=2 * 512 * 2304 * 1024, nbytes=12 << 20,
    )
    projected, _ = scatter_pair(m_mine, m_part)
    mlp_scale = norm_scale(projected)
    mlp_hat = projected * mlp_scale
    output = (hidden_state + mlp_hat * gain_mlp).astype(BF16)[None]

    upstream = out_grad[0].astype(F32)
    grad_gain_mlp = jnp.sum(upstream * mlp_hat, axis=0)
    d_projected = norm_back(upstream * gain_mlp, mlp_hat, mlp_scale).astype(BF16)
    n = jnp.arange(1024, dtype=jnp.int32)
    source = ((n // 8) % 16) * 64 + (n // 128) * 8 + n % 8
    order = (n[None, :] == source[:, None]).astype(BF16)
    h_turned = dot_nt(order, h_all).astype(BF16)
    d_blocks = gather_pair(d_projected)
    d_blocks[3], h_turned = lax.optimization_barrier((d_blocks[3], h_turned))
    dm_all, d_gu, dh_mine, dh_part = kernel_call(
        expand_back_body,
        [
            0, shaped((512, 1536), BF16), shaped((256, 1024), F32), shaped((256, 1024), BF16),
        ],
        [d_blocks, gate, up, w_mlp, w_down_rows],
        flops=2 * 512 * 2304 * 1024, nbytes=12 << 20,
    )

    far = dh_mine[128:] + swap(dh_part[128:], CORE_SWAP).astype(F32)
    far, d_gu, dm_all = lax.optimization_barrier((far.astype(BF16), d_gu, dm_all))
    far = swap(far, Z_SWAP)
    (grad_mlp,) = kernel_call(
        expand_grad_body,
        in_hbm(shaped((1024, 2304), BF16)),
        [h_turned, d_gu, expanded, dm_all],
        [pltpu.VMEM((768, 512), BF16)],
        flops=2 * 512 * 2304 * 1024, nbytes=9 << 20,
    )
    far, grad_mlp = lax.optimization_barrier((far, grad_mlp))
    grad_mlp = lax.psum_scatter(grad_mlp, "fsdp", scatter_dimension=0, tiled=True)
    d_hidden = upstream + dh_mine[:128] + swap(dh_part[:128], CORE_SWAP).astype(F32)
    d_hidden = d_hidden + far.astype(F32)

    grad_gain_attn = jnp.sum(d_hidden * attn_hat, axis=0)
    d_attended = norm_back(d_hidden * gain_attn, attn_hat, attn_scale).astype(BF16)
    d_tiles, deltas, grad_out = kernel_call(
        output_back_body,
        [shaped((8, 256, 128), BF16), shaped((8, 2, 128), F32), shaped((256, 1024), BF16)],
        [place, *in_hbm(out_raw, w_out_rows, gather_group(d_attended), mixed_turned)],
        flops=4 * 1024 * 1024 * 256, nbytes=6 << 20,
    )
    dq, dk, dv, d_low, dots = kernel_call(
        attend_back_body,
        [
            *in_hbm(
                shaped((1024, 256), BF16), shaped((1024, 128), F32), shaped((1024, 128), F32),
                shaped((1024, 256), BF16),
            ),
            shaped((24, 128), F32),
        ],
        [place, *in_hbm(q_tiles, keys, vals), logs, d_tiles, deltas],
        [
            pltpu.VMEM((128, 2048), BF16), pltpu.VMEM((2048, 128), F32),
            pltpu.VMEM((2048, 128), F32),
        ],
        flops=10 * 1024 * 2048 * 256, nbytes=8 << 20,
    )
    fsdp = lax.axis_index("fsdp")
    def halve(value, rows, bit, axis, pairs):
        parts = value.reshape(-1, 2, rows, 1024)
        given = jnp.where(bit == 1, parts[:, 0], parts[:, 1])
        mine = jnp.where(bit == 1, parts[:, 1], parts[:, 0]).astype(F32)
        return (mine + lax.ppermute(given, axis, pairs).astype(F32)).astype(BF16)

    grad_out = halve(grad_out, 32, fsdp % 2, "fsdp", [(i, i ^ 1) for i in range(8)])
    d_got = swap(d_low, HIGH_TO_LOW)
    dots = sum_group(dots)
    dots_got = swap(dots[16:], HIGH_TO_LOW)

    gains = jnp.concatenate([grad_gain_attn.reshape(128, 8), grad_gain_mlp.reshape(128, 8)], axis=1)
    gains = jnp.broadcast_to(
        jnp.pad(gains.astype(BF16), ((0, 0), (24, 88)))[:, None, :], (128, 8, 128)
    ).reshape(1024, 128)
    d_made, sent = kernel_call(
        unproject_body,
        [shaped((1024, 512), BF16), shaped((1024, 640), BF16)],
        [
            place, *in_hbm(dq, dk, dv), d_got, *in_hbm(q_raw, k_raw), squares, dots, dots_got, cosine, sine,
            gain_q, gain_k, *in_hbm(x_turned), gains,
        ],
        [pltpu.VMEM((8, 384), F32)],
        flops=2 * 1024 * 1024 * 512, nbytes=9 << 20,
    )

    def halves(value, upper):
        low, high = value[: value.shape[0] // 2], value[value.shape[0] // 2 :]
        return jnp.where(upper, high, low), jnp.where(upper, low, high)

    mine, given = halves(grad_mlp, xh == 1)
    mine = mine.astype(F32) + swap(given, X_SWAP).astype(F32)
    grad_out = after(grad_out, sent)
    grad_out = halve(grad_out, 32, fsdp // 2 % 2, "fsdp", [(i, i ^ 2) for i in range(8)])
    grad_out = halve(grad_out, 32, fsdp // 4, "fsdp", [(i, i ^ 4) for i in range(8)])
    got_made = lax.all_to_all(
        sent.reshape(128, 8, 640), ("seq", "fsdp"), split_axis=0, concat_axis=0, tiled=True
    )
    dx_mine, dx_part = kernel_call(
        input_body,
        [shaped((512, 1024), F32), shaped((512, 1024), BF16)],
        [after(d_made, sent), weight],
        flops=2 * 1024 * 1024 * 512, nbytes=5 << 20,
    )
    rows = [slice(k * 128, k * 128 + 128) for k in range(4)]
    pieces = [dx_mine[r] + swap(dx_part[r], CORE_SWAP).astype(F32) for r in rows]
    far = [piece.astype(BF16) for piece in pieces[1:]]
    d_inputs = pieces[0] + sum(
        swap(piece, to_z(k)).astype(F32) for k, piece in enumerate(far, 1)
    )
    grad_down = jnp.concatenate(
        [
            mine[:48, 1536:2304],
            jnp.concatenate([mine[48:, 1536 + m * 256 : 1792 + m * 256] for m in range(3)], axis=0),
        ],
        axis=1,
    )
    grad_down, given_down = halves(grad_down, z >= 2)
    mine, given = halves(mine[:, :1536], z >= 2)
    given = swap(
        jnp.concatenate([given.reshape(48, 1024), given_down], axis=0).astype(BF16), FAR_SWAP
    ).astype(F32)
    mine = (mine + given[:48].reshape(32, 1536)).astype(BF16)
    grad_down = (grad_down + given[48:]).astype(BF16)

    got_made, mine, grad_down, grad_out, d_inputs = lax.optimization_barrier(
        (got_made, mine, grad_down, grad_out, d_inputs)
    )
    grad_out = halve(grad_out, 16, xh, "seq", X_SWAP)
    grad_out = swap(grad_out.reshape(16, 1024), OUT_HOME)
    grad_down = lax.ppermute(grad_down, ("seq", "fsdp"), DOWN_HOME)
    mine, given = halves(mine, z % 2 == 1)
    got = swap(given, Z_SWAP)
    mine = jnp.stack([jnp.where(z % 2 == 1, got, mine), jnp.where(z % 2 == 1, mine, got)])
    mine = mine.reshape(2, 2, 8, 1536)
    given = jnp.where(c == 1, mine[:, 0], mine[:, 1])
    mine = jnp.where(c == 1, mine[:, 1], mine[:, 0])
    got = swap(given, CORE_SWAP)
    got_wide = jnp.stack([jnp.where(c == 1, got, mine), jnp.where(c == 1, mine, got)], axis=1)
    summed = jnp.sum(got_made.reshape(2, 8, 8, 8, 640).astype(F32), axis=(0, 2))
    gains = jnp.sum(summed[:, 0, 512:], axis=0)

    def take(first, width):
        return summed[:, :, first : first + width].swapaxes(0, 1).reshape(8, 8 * width)

    wide = got_wide.astype(F32).reshape(4, 8, 2, 8, 96)
    wide = wide.transpose(2, 1, 3, 0, 4).reshape(2, 8, 3072)
    return (
        output,
        (d_hidden + d_inputs).astype(BF16)[None],
        take(0, 256),
        take(256, 128),
        take(384, 128),
        grad_out.astype(F32),
        wide[0],
        wide[1],
        grad_down.astype(F32),
        gains[:16],
        gains[16:24],
        gains[24:32],
        gains[32:40],
    )


def solution(mesh):
    rows = P("fsdp", "seq", None)
    weight = P("fsdp", None)
    grad = P(("seq", "fsdp"), None)
    gain = P(("seq", "fsdp"))
    return jax.shard_map(
        on_device,
        mesh=mesh,
        in_specs=(rows,) * 2 + (weight,) * 7 + (P(),) * 4,
        out_specs=(rows,) * 2 + (grad,) * 7 + (gain,) * 4,
        check_vma=False,
    )
```

profile of v0, /device:TPU:6, one launch (start us, length us, event | category | flops | bytes accessed | tf_op | source)
XLA Modules:
  0.0 351.9 jit_solution(10837284176356036757)
XLA Ops:
  7.2 4.1 %collective-permute-start = (bf16[128,1024]{1,0:T(8,128)(2,1)}, bf16[128,1024]{1,0:T(8,128)(2,1)S(1)}, u32[]{:S(2)}, u32[]{:S(2)}) collective-permute-start(bf16[128,1024]{1,0:T(8,128)(2,1)} %bitcast.144), channel_id=1, source_target_pairs={{16,0},{24,8},{32,16},{40,24},{48,32},{56,40},{0,48},{8,56},{80,64... | collective-permute-start | bytes 786440 | tf_op jit(solution)/shard_map/ppermute | solution.py:64
  14.5 5.9 %all-to-all-start = ((bf16[8,128,512]{2,1,0:T(8,128)(2,1)}), bf16[8,128,512]{2,1,0:T(8,128)(2,1)S(1)}, u32[]{:S(2)}, u32[]{:S(2)}) async-start(bf16[8,128,512]{2,1,0:T(8,128)(2,1)} %broadcast_in_dim.14), calls=%async_computation | async-start | bytes 2097152 | tf_op jit(solution)/shard_map/all_to_all | solution.py:682
  42.1 4.3 %collective-permute-done.7 = bf16[32,1024]{1,0:T(8,128)(2,1)S(1)} collective-permute-done((bf16[32,1024]{1,0:T(8,128)(2,1)S(1)}, bf16[32,1024]{1,0:T(8,128)(2,1)S(1)}, u32[]{:S(2)}, u32[]{:S(2)}) %collective-permute-start.7) | collective-permute-done | bytes 65568 | tf_op jit(solution)/shard_map/ppermute | solution.py:693
  46.5 5.5 %shard_map.228 = (bf16[1024,1024]{1,0:T(8,128)(2,1)}, f32[1024,256]{1,0:T(8,128)}, f32[1024,128]{1,0:T(8,128)}, bf16[1024,256]{1,0:T(8,128)(2,1)}, bf16[1024,256]{1,0:T(8,128)(2,1)}, /*index=5*/f32[16,128]{1,0:T(8,128)S(1)}) custom-call(bf16[128,1024]{1,0:T(8,128)(2,1)S(1)} %bitcast.148, bf16[128,1024]{1,0:T(8,128)(2,1)S(1)} %collective-permute-done.refs_1_, ...), custom_call_target="tpu_custom_call" | custom-call | flops 1073741824 | bytes 9437184 | tf_op jit(solution)/shard_map/pallas_call | solution.py:217
  64.8 23.0 %collective-permute-done.12.refs_5_ = f32[8,128]{1,0:T(8,128)S(1)} collective-permute-done((f32[8,128]{1,0:T(8,128)S(1)}, f32[8,128]{1,0:T(8,128)S(1)}, u32[]{:S(2)}, u32[]{:S(2)}) %collective-permute-start.12) | collective-permute-done | bytes 4128 | tf_op jit(solution)/shard_map/ppermute | solution.py:64
  88.7 6.6 %all-to-all-start.1 = ((bf16[8,32,1024]{2,1,0:T(8,128)(2,1)}), bf16[8,32,1024]{2,1,0:T(8,128)(2,1)S(1)}, u32[]{:S(2)}, u32[]{:S(2)}) async-start(bf16[8,32,1024]{2,1,0:T(8,128)(2,1)} %broadcast_in_dim.17), calls=%async_computation.1 | async-start | bytes 1048576 | tf_op jit(solution)/shard_map/all_to_all | solution.py:682
  95.4 11.9 %shard_map.229 = (f32[1024,256]{1,0:T(8,128)}, bf16[1024,256]{1,0:T(8,128)(2,1)}, bf16[256,1024]{1,0:T(8,128)(2,1)}, bf16[8,256,128]{2,1,0:T(8,128)(2,1)}, bf16[...) custom-call(s32[3]{0:T(128)S(1)} %pad_add_fusion.refs_0_, ...), custom_call_target="tpu_custom_call" | custom-call | flops 2147483648 | bytes 9437184 | tf_op jit(solution)/shard_map/pallas_call | solution.py:217
  121.8 4.0 %copy.71 = bf16[1024,1024]{0,1:T(8,128)(2,1)} copy(bf16[1024,1024]{1,0:T(8,128)(2,1)} %get-tuple-element.83) | data formatting | bytes 4194304 | tf_op jit(solution)/shard_map/pallas_call | solution.py:217
  127.3 4.8 %collective-permute-done.16 = bf16[128,1024]{1,0:T(8,128)(2,1)S(1)} collective-permute-done((bf16[128,1024]{1,0:T(8,128)(2,1)S(1)}, bf16[128,1024]{1,0:T(8,128)(2,1)S(1)}, u32[]{:S(2)}, u32[]{:S(2)}) %collective-permute-start.16) | collective-permute-done | bytes 262176 | tf_op jit(solution)/shard_map/ppermute | solution.py:64
  135.6 7.9 %collective-permute-done.20.refs_1_ = bf16[128,1024]{1,0:T(8,128)(2,1)S(1)} collective-permute-done((bf16[128,1024]{1,0:T(8,128)(2,1)S(1)}, bf16[128,1024]{1,0:T(8,128)(2,1)S(1)}, u32[]{:S(2)}, u32[]{:S(2)}) %collective-permute-start.20) | collective-permute-done | bytes 262176 | tf_op jit(solution)/shard_map/ppermute | solution.py:64
  145.1 7.0 %shard_map.231 = (bf16[512,1024]{1,0:T(8,128)(2,1)S(1)}, f32[512,768]{1,0:T(8,128)S(1)}, f32[512,768]{1,0:T(8,128)S(1)}, bf16[512,768]{1,0:T(8,128)(2,1)S(1)}, f...) custom-call(bf16[128,1024]{1,0:T(8,128)(2,1)S(1)} %fusion.12.refs_0_, ...), custom_call_target="tpu_custom_call" | custom-call | flops 2415919104 | bytes 12582912 | tf_op jit(solution)/shard_map/pallas_call | solution.py:217
  154.2 8.1 %collective-permute-done.25 = bf16[128,1024]{1,0:T(8,128)(2,1)S(1)} collective-permute-done((bf16[128,1024]{1,0:T(8,128)(2,1)S(1)}, bf16[128,1024]{1,0:T(8,128)(2,1)S(1)}, u32[]{:S(2)}, u32[]{:S(2)}) %collective-permute-start.25) | collective-permute-done | bytes 262176 | tf_op jit(solution)/shard_map/ppermute | solution.py:64
  163.3 7.2 %collective-permute-done.26.refs_1_ = bf16[128,1024]{1,0:T(8,128)(2,1)S(1)} collective-permute-done((bf16[128,1024]{1,0:T(8,128)(2,1)S(1)}, bf16[128,1024]{1,0:T(8,128)(2,1)S(1)}, u32[]{:S(2)}, u32[]{:S(2)}) %collective-permute-start.26) | collective-permute-done | bytes 262176 | tf_op jit(solution)/shard_map/ppermute | solution.py:64
  172.1 5.2 %shard_map.232 = (bf16[512,1024]{1,0:T(8,128)(2,1)S(1)}, bf16[512,1536]{1,0:T(8,128)(2,1)S(1)}, f32[256,1024]{1,0:T(8,128)S(1)}, bf16[256,1024]{1,0:T(8,128)(2,1)S(1)}) custom-call(bf16[128,1024]{1,0:T(8,128)(2,1)S(1)} %fusion.7.refs_0_, bf16[128,1024]{1,0:T(8,128)(2,1)S(1)} %collective-permute-done.26.refs_1_, ...), custom_call_target="tpu_custom_call" | custom-call | flops 2415919104 | bytes 12582912 | tf_op jit(solution)/shard_map/pallas_call | solution.py:217
  180.6 6.4 %shard_map.233 = bf16[1024,2304]{1,0:T(8,128)(2,1)} custom-call(bf16[1024,512]{1,0:T(8,128)(2,1)S(1)} %fusion.2.refs_0_, bf16[512,1536]{1,0:T(8,128)(2,1)S(1)} %get-tuple-element.100.refs_1_, bf16[512,768]{1,0:T(8,128)(2,1)S(1)} %get-tuple-element.101.refs_2_, bf16[512,1024]{1,0:T(8,128)(2,1)S(1)} %get-tuple-element.102.refs_3_), custom_call_target="tpu_custom_call" | custom-call | flops 2415919104 | bytes 9437184 | tf_op jit(solution)/shard_map/pallas_call | solution.py:217
  196.5 10.4 %collective-permute-done.32.refs_4_ = bf16[128,1024]{1,0:T(8,128)(2,1)S(1)} collective-permute-done((bf16[128,1024]{1,0:T(8,128)(2,1)S(1)}, bf16[128,1024]{1,0:T(8,128)(2,1)S(1)}, u32[]{:S(2)}, u32[]{:S(2)}) %collective-permute-start.32) | collective-permute-done | bytes 262176 | tf_op jit(solution)/shard_map/ppermute | solution.py:64
  212.2 5.1 %shard_map.234 = (bf16[8,256,128]{2,1,0:T(8,128)(2,1)S(1)}, f32[8,2,128]{2,1,0:T(2,128)S(1)}, bf16[256,1024]{1,0:T(8,128)(2,1)S(1)}) custom-call(s32[3]{0:T(128)S(1)} %pad_add_fusion.refs_0_, f32[1024,256]{1,0:T(8,128)} %get-tuple-element.108.refs_1_, bf16[256,1024]{1,0:T(8,128)(2,1)} %bitcast.150, bf16[128,1024]{1,0:T(8,128)(2,1)} %copy-done.18, ...), custom_call_target="tpu_custom_call" | custom-call | flops 1073741824 | bytes 6291456 | tf_op jit(solution)/shard_map/pallas_call | solution.py:217
  217.3 16.3 %shard_map.235 = (bf16[1024,256]{1,0:T(8,128)(2,1)}, f32[1024,128]{1,0:T(8,128)}, f32[1024,128]{1,0:T(8,128)}, bf16[1024,256]{1,0:T(8,128)(2,1)}, f32[24,128]{1,0:T(8,128)S(1)}) custom-call(s32[3]{0:T(128)S(1)} %pad_add_fusion.refs_0_, bf16[8,256,128]{2,1,0:T(8,128)(2,1)} %get-tuple-element.104.refs_1_, bf16[2048,128]{1,0:T(8,128)(2,1)} %get-tuple-element.105.refs_2_, ...), custom_call_target="tpu_custom_call" | custom-call | flops 5368709120 | bytes 8388608 | tf_op jit(solution)/shard_map/pallas_call | solution.py:217
  239.5 4.5 %collective-permute-done.42 = f32[3,2,4,128]{3,2,1,0:T(4,128)S(1)} collective-permute-done((f32[3,2,4,128]{3,2,1,0:T(4,128)S(1)}, f32[3,2,4,128]{3,2,1,0:T(4,128)S(1)}, u32[]{:S(2)}, u32[]{:S(2)}) %collective-permute-start.42) | collective-permute-done | bytes 12320 | tf_op jit(solution)/shard_map/ppermute | solution.py:64
  252.3 7.3 %shard_map.236 = (bf16[1024,512]{1,0:T(8,128)(2,1)S(1)}, bf16[1024,640]{1,0:T(8,128)(2,1)}) custom-call(s32[3]{0:T(128)S(1)} %pad_add_fusion.refs_0_, bf16[1024,256]{1,0:T(8,128)(2,1)} %get-tuple-element.112.refs_1_, f32[1024,128]{1,0:T(8,128)} %get-tuple-element.113.refs_2_, f32[1024,128]{1,0:T(8,128)} %get-tuple-element.114.refs_3_, ...), custom_call_target="tpu_custom_call" | custom-call | flops 1073741824 | bytes 9437184 | tf_op jit(solution)/shard_map/pallas_call | solution.py:217
  265.1 10.9 %all-to-all-start.2 = ((bf16[128,8,640]{2,1,0:T(8,128)(2,1)}), bf16[128,8,640]{2,1,0:T(8,128)(2,1)S(1)}, u32[]{:S(2)}, u32[]{:S(2)}) async-start(bf16[128,8,640]{2,1,0:T(8,128)(2,1)} %bitcast.30), calls=%async_computation.2 | async-start | bytes 2621440 | tf_op jit(solution)/shard_map/all_to_all | solution.py:870
  279.7 13.1 %collective-permute-done.48 = bf16[1,32,1024]{2,1,0:T(8,128)(2,1)} collective-permute-done((bf16[1,32,1024]{2,1,0:T(8,128)(2,1)}, bf16[1,32,1024]{2,1,0:T(8,128)(2,1)}, u32[]{:S(2)}, u32[]{:S(2)}) %collective-permute-start.48) | collective-permute-done | bytes 65568 | tf_op jit(solution)/shard_map/ppermute | solution.py:839
  326.6 5.6 %collective-permute-start.60 = (bf16[24,1024]{1,0:T(8,128)(2,1)S(1)}, bf16[24,1024]{1,0:T(8,128)(2,1)S(1)}, u32[]{:S(2)}, u32[]{:S(2)}) collective-permute-start(bf16[24,1024]{1,0:T(8,128)(2,1)S(1)} %fusion.21), channel_id=1, source_target_pairs={{0,0},{1,16},{2,32},{3,48},{4,64},{5,80},{6,96},{7,112},{8,4},{9,2... | collective-permute-start | bytes 147464 | tf_op jit(solution)/shard_map/ppermute | solution.py:905
  336.3 5.8 %collective-permute-done.57 = bf16[16,1024]{1,0:T(8,128)(2,1)S(1)} collective-permute-done((bf16[16,1024]{1,0:T(8,128)(2,1)S(1)}, bf16[16,1024]{1,0:T(8,128)(2,1)S(1)}, u32[]{:S(2)}, u32[]{:S(2)}) %collective-permute-start.57) | collective-permute-done | bytes 32800 | tf_op jit(solution)/shard_map/ppermute | solution.py:64
  (298 shorter events, 145.8 us)
Async XLA Ops:
  7.2 26.6 %collective-permute-start = (bf16[128,1024]{1,0:T(8,128)(2,1)}, bf16[128,1024]{1,0:T(8,128)(2,1)S(1)}, u32[]{:S(2)}, u32[]{:S(2)}) collective-permute-start(bf16[128,1024]{1,0:T(8,128)(2,1)} %bitcast.144), channel_id=1, source_target_pairs={{16,0},{24,8},{32,16},{40,24},{48,32},{56,40},{0,48},{8,56},{80,64... | collective-permute-start | bytes 786440 | tf_op jit(solution)/shard_map/ppermute | solution.py:64
  11.3 22.5 %collective-permute-start.1 = (bf16[128,1024]{1,0:T(8,128)(2,1)}, bf16[128,1024]{1,0:T(8,128)(2,1)S(1)}, u32[]{:S(2)}, u32[]{:S(2)}) collective-permute-start(bf16[128,1024]{1,0:T(8,128)(2,1)} %bitcast.145), channel_id=1, source_target_pairs={{32,0},{40,8},{48,16},{56,24},{0,32},{8,40},{16,48},{24,56},{96,64... | collective-permute-start | bytes 786440 | tf_op jit(solution)/shard_map/ppermute | solution.py:64
  11.3 23.1 %collective-permute-start.2 = (bf16[128,1024]{1,0:T(8,128)(2,1)}, bf16[128,1024]{1,0:T(8,128)(2,1)S(1)}, u32[]{:S(2)}, u32[]{:S(2)}) collective-permute-start(bf16[128,1024]{1,0:T(8,128)(2,1)} %bitcast.146), channel_id=1, source_target_pairs={{48,0},{56,8},{0,16},{8,24},{16,32},{24,40},{32,48},{40,56},{112,6... | collective-permute-start | bytes 786440 | tf_op jit(solution)/shard_map/ppermute | solution.py:64
  12.6 33.9 %collective-permute-start.3 = (bf16[128,1024]{1,0:T(8,128)(2,1)}, bf16[128,1024]{1,0:T(8,128)(2,1)S(1)}, u32[]{:S(2)}, u32[]{:S(2)}) collective-permute-start(bf16[128,1024]{1,0:T(8,128)(2,1)} %bitcast.147), channel_id=1, source_target_pairs={{0,8},{8,0},{16,24},{24,16},{32,40},{40,32},{48,56},{56,48},{64,72... | collective-permute-start | bytes 786440 | tf_op jit(solution)/shard_map/ppermute | solution.py:64
  14.5 32.0 %all-to-all-start = ((bf16[8,128,512]{2,1,0:T(8,128)(2,1)}), bf16[8,128,512]{2,1,0:T(8,128)(2,1)S(1)}, u32[]{:S(2)}, u32[]{:S(2)}) async-start(bf16[8,128,512]{2,1,0:T(8,128)(2,1)} %broadcast_in_dim.14), calls=%async_computation | async-start | bytes 2097152 | tf_op jit(solution)/shard_map/all_to_all | solution.py:682
  20.4 124.7 %all-gather.2.cloned.1.call-start = ((), (), s32[]{:S(2)}) async-start(), calls=%async_computation.4 | async-start | bytes 5308416 | tf_op jit(solution)/shard_map/all_gather | solution.py:731
  58.8 36.6 %collective-permute-start.8 = (bf16[1024,256]{1,0:T(8,128)(2,1)}, bf16[1024,256]{1,0:T(8,128)(2,1)S(1)}, u32[]{:S(2)}, u32[]{:S(2)}) collective-permute-start(bf16[1024,256]{1,0:T(8,128)(2,1)} %get-tuple-element.76.refs_2_), channel_id=1, source_target_pairs={{0,64},{8,72},{16,80},{24,88},{32,96},{40,104},{48,112},{56,120},{... | collective-permute-start | bytes 1572872 | tf_op jit(solution)/shard_map/ppermute | solution.py:64
  63.4 24.4 %collective-permute-start.12 = (f32[8,128]{1,0:T(8,128)S(1)}, f32[8,128]{1,0:T(8,128)S(1)}, u32[]{:S(2)}, u32[]{:S(2)}) collective-permute-start(f32[8,128]{1,0:T(8,128)S(1)} %bitcast.179), channel_id=1, source_target_pairs={{0,64},{8,72},{16,80},{24,88},{32,96},{40,104},{48,112},{56,120},{... | collective-permute-start | bytes 12296 | tf_op jit(solution)/shard_map/ppermute | solution.py:64
  88.7 20.7 %all-to-all-start.1 = ((bf16[8,32,1024]{2,1,0:T(8,128)(2,1)}), bf16[8,32,1024]{2,1,0:T(8,128)(2,1)S(1)}, u32[]{:S(2)}, u32[]{:S(2)}) async-start(bf16[8,32,1024]{2,1,0:T(8,128)(2,1)} %broadcast_in_dim.17), calls=%async_computation.1 | async-start | bytes 1048576 | tf_op jit(solution)/shard_map/all_to_all | solution.py:682
  95.3 183.3 %reduce-scatter.2.cloned.1.call-start = ((), (), s32[]{:S(2)}) async-start(), calls=%async_computation.5 | async-start | bytes 5308416 | tf_op jit(solution)/shard_map/reduce_scatter | solution.py:806
  118.2 13.9 %collective-permute-start.16 = (bf16[128,1024]{1,0:T(8,128)(2,1)S(1)}, bf16[128,1024]{1,0:T(8,128)(2,1)S(1)}, u32[]{:S(2)}, u32[]{:S(2)}) collective-permute-start(bf16[128,1024]{1,0:T(8,128)(2,1)S(1)} %get-tuple-element.148), channel_id=1, source_target_pairs={{0,16},{8,24},{16,32},{24,40},{32,48},{40,56},{48,0},{56,8},{64,80... | collective-permute-start | bytes 786440 | tf_op jit(solution)/shard_map/ppermute | solution.py:64
  193.5 13.4 %collective-permute-start.32 = (bf16[128,1024]{1,0:T(8,128)(2,1)S(1)}, bf16[128,1024]{1,0:T(8,128)(2,1)S(1)}, u32[]{:S(2)}, u32[]{:S(2)}) collective-permute-start(bf16[128,1024]{1,0:T(8,128)(2,1)S(1)} %get-tuple-element.163.refs_3_), channel_id=1, source_target_pairs={{16,0},{24,8},{32,16},{40,24},{48,32},{56,40},{0,48},{8,56},{80,64... | collective-permute-start | bytes 786440 | tf_op jit(solution)/shard_map/ppermute | solution.py:64
  195.9 14.6 %collective-permute-start.34 = (bf16[128,1024]{1,0:T(8,128)(2,1)S(1)}, bf16[128,1024]{1,0:T(8,128)(2,1)S(1)}, u32[]{:S(2)}, u32[]{:S(2)}) collective-permute-start(bf16[128,1024]{1,0:T(8,128)(2,1)S(1)} %get-tuple-element.163.refs_3_), channel_id=1, source_target_pairs={{48,0},{56,8},{0,16},{8,24},{16,32},{24,40},{32,48},{40,56},{112,6... | collective-permute-start | bytes 786440 | tf_op jit(solution)/shard_map/ppermute | solution.py:64
  196.5 14.4 %collective-permute-start.35 = (bf16[128,1024]{1,0:T(8,128)(2,1)S(1)}, bf16[128,1024]{1,0:T(8,128)(2,1)S(1)}, u32[]{:S(2)}, u32[]{:S(2)}) collective-permute-start(bf16[128,1024]{1,0:T(8,128)(2,1)S(1)} %get-tuple-element.163.refs_3_), channel_id=1, source_target_pairs={{0,8},{8,0},{16,24},{24,16},{32,40},{40,32},{48,56},{56,48},{64,72... | collective-permute-start | bytes 786440 | tf_op jit(solution)/shard_map/ppermute | solution.py:64
  235.0 17.3 %collective-permute-start.39 = (bf16[1024,256]{1,0:T(8,128)(2,1)}, bf16[1024,256]{1,0:T(8,128)(2,1)S(1)}, u32[]{:S(2)}, u32[]{:S(2)}) collective-permute-start(bf16[1024,256]{1,0:T(8,128)(2,1)} %get-tuple-element.115), channel_id=1, source_target_pairs={{64,0},{72,8},{80,16},{88,24},{96,32},{104,40},{112,48},{120,56},{... | collective-permute-start | bytes 1572872 | tf_op jit(solution)/shard_map/ppermute | solution.py:64
  259.7 16.4 %collective-permute-start.47 = (bf16[2,32,1024]{2,1,0:T(8,128)(2,1)S(1)}, bf16[2,32,1024]{2,1,0:T(8,128)(2,1)}, u32[]{:S(2)}, u32[]{:S(2)}) collective-permute-start(bf16[2,32,1024]{2,1,0:T(8,128)(2,1)S(1)} %select_bitcast_fusion), channel_id=1, source_target_pairs={{0,2},{1,3},{2,0},{3,1},{4,6},{5,7},{6,4},{7,5},{8,10},{9,11},{10,... | collective-permute-start | bytes 393224 | tf_op jit(solution)/shard_map/ppermute | solution.py:839
  264.0 31.2 %collective-permute-start.50 = (bf16[128,1024]{1,0:T(8,128)(2,1)}, bf16[128,1024]{1,0:T(8,128)(2,1)}, u32[]{:S(2)}, u32[]{:S(2)}) collective-permute-start(bf16[128,1024]{1,0:T(8,128)(2,1)} %get-tuple-element.152), channel_id=1, source_target_pairs={{0,8},{8,0},{16,24},{24,16},{32,40},{40,32},{48,56},{56,48},{64,72... | collective-permute-start | bytes 786440 | tf_op jit(solution)/shard_map/ppermute | solution.py:64
  264.0 31.2 %collective-permute-start.52 = (bf16[128,1024]{1,0:T(8,128)(2,1)}, bf16[128,1024]{1,0:T(8,128)(2,1)}, u32[]{:S(2)}, u32[]{:S(2)}) collective-permute-start(bf16[128,1024]{1,0:T(8,128)(2,1)} %get-tuple-element.151), channel_id=1, source_target_pairs={{0,8},{8,0},{16,24},{24,16},{32,40},{40,32},{48,56},{56,48},{64,72... | collective-permute-start | bytes 786440 | tf_op jit(solution)/shard_map/ppermute | solution.py:64
  264.5 30.7 %collective-permute-start.54 = (bf16[128,1024]{1,0:T(8,128)(2,1)}, bf16[128,1024]{1,0:T(8,128)(2,1)}, u32[]{:S(2)}, u32[]{:S(2)}) collective-permute-start(bf16[128,1024]{1,0:T(8,128)(2,1)} %get-tuple-element.150), channel_id=1, source_target_pairs={{0,8},{8,0},{16,24},{24,16},{32,40},{40,32},{48,56},{56,48},{64,72... | collective-permute-start | bytes 786440 | tf_op jit(solution)/shard_map/ppermute | solution.py:64
  264.6 50.6 %collective-permute-start.49 = (bf16[128,1024]{1,0:T(8,128)(2,1)}, bf16[128,1024]{1,0:T(8,128)(2,1)}, u32[]{:S(2)}, u32[]{:S(2)}) collective-permute-start(bf16[128,1024]{1,0:T(8,128)(2,1)} %get-tuple-element.149), channel_id=1, source_target_pairs={{0,8},{8,0},{16,24},{24,16},{32,40},{40,32},{48,56},{56,48},{64,72... | collective-permute-start | bytes 786440 | tf_op jit(solution)/shard_map/ppermute | solution.py:64
  265.1 56.5 %all-to-all-start.2 = ((bf16[128,8,640]{2,1,0:T(8,128)(2,1)}), bf16[128,8,640]{2,1,0:T(8,128)(2,1)S(1)}, u32[]{:S(2)}, u32[]{:S(2)}) async-start(bf16[128,8,640]{2,1,0:T(8,128)(2,1)} %bitcast.30), calls=%async_computation.2 | async-start | bytes 2621440 | tf_op jit(solution)/shard_map/all_to_all | solution.py:870
  277.8 15.0 %collective-permute-start.48 = (bf16[1,32,1024]{2,1,0:T(8,128)(2,1)}, bf16[1,32,1024]{2,1,0:T(8,128)(2,1)}, u32[]{:S(2)}, u32[]{:S(2)}) collective-permute-start(bf16[1,32,1024]{2,1,0:T(8,128)(2,1)} %select_bitcast_fusion.1), channel_id=1, source_target_pairs={{0,4},{1,5},{2,6},{3,7},{4,0},{5,1},{6,2},{7,3},{8,12},{9,13},{10,... | collective-permute-start | bytes 196616 | tf_op jit(solution)/shard_map/ppermute | solution.py:839
  297.4 17.7 %collective-permute-start.51 = (bf16[128,1024]{1,0:T(8,128)(2,1)}, bf16[128,1024]{1,0:T(8,128)(2,1)}, u32[]{:S(2)}, u32[]{:S(2)}) collective-permute-start(bf16[128,1024]{1,0:T(8,128)(2,1)} %get-tuple-element.143), channel_id=1, source_target_pairs={{0,16},{8,24},{16,32},{24,40},{32,48},{40,56},{48,0},{56,8},{64,80... | collective-permute-start | bytes 786440 | tf_op jit(solution)/shard_map/ppermute | solution.py:64
  299.2 15.9 %collective-permute-start.53 = (bf16[128,1024]{1,0:T(8,128)(2,1)}, bf16[128,1024]{1,0:T(8,128)(2,1)}, u32[]{:S(2)}, u32[]{:S(2)}) collective-permute-start(bf16[128,1024]{1,0:T(8,128)(2,1)} %get-tuple-element.145), channel_id=1, source_target_pairs={{0,32},{8,40},{16,48},{24,56},{32,0},{40,8},{48,16},{56,24},{64,96... | collective-permute-start | bytes 786440 | tf_op jit(solution)/shard_map/ppermute | solution.py:64
  (73 other events, 505.5 us)
Sparse Core Ops, SparseCore 0:
  52.1 63.4 all-gather.1
  189.3 60.8 reduce-scatter.1
where the time goes:
time: 359 us; the launch traced here: 352 us
  waiting for transfers between devices  124 us (35%)
  starting transfers between devices  79.4 us (22%)
  Pallas kernels  68.9 us (19%)
  local copies, waits for them, and re-layouts  31.8 us (9%)
  other arithmetic  30.9 us (9%)
  between operations  15.4 us (4%)
    ppermute x55, waiting for transfers between devices, swap(): return lax.ppermute(value, 'seq', pairs)  101 us
    pallas_call x10, Pallas kernels, kernel_call(): pl.pallas_call(whole, out_shape=tuple(shapes), in_specs=[where(s) for gro...  68.9 us
    ppermute x55, starting transfers between devices, swap(): return lax.ppermute(value, 'seq', pairs)  42.8 us
    ppermute x4, waiting for transfers between devices, halve(): return (mine + lax.ppermute(given, axis, pairs).astype(F32)).astype(BF16)  16.3 us
    all_to_all x2, starting transfers between devices, spread(): lax.all_to_all(jnp.broadcast_to(block[None], (8,) + block.shape), 'fsdp',...  12.6 us
    all_to_all x1, starting transfers between devices, on_device(): lax.all_to_all(sent.reshape(128, 8, 640), ('seq', 'fsdp'), split_axis=0,...  10.9 us
    unnamed x65, local copies, waits for them, and re-layouts  7.53 us
  transfers between devices with their start and end apart: 66, of which 31 were waited for; matrix products, arithmetic and copies ran while one was open for 16% of the time, Pallas kernels for 15%

commit v1 on v0

--- a/solution.py
+++ b/solution.py
@@ -54,10 +54,13 @@
 Z_SWAP = [(i, i ^ 2) for i in range(16)]
 FAR_SWAP = [(i, i ^ 4) for i in range(16)]
 OUT_HOME = [(xh * 8 + a, 2 * a + xh) for xh in range(2) for a in range(8)]
-DOWN_HOME = across(
-    (seq_index(xh, 2 * zh + zl, c), f, 2 * f + zl, 4 * c + 2 * xh + zh)
-    for xh in range(2) for zh in range(2) for zl in range(2) for c in range(2) for f in range(8)
-)
+
+
+def down_home(other):
+    return across(
+        (seq_index(xh, 2 * zh + zl, c), f, 2 * f + zl, 4 * c + 2 * xh + (zh ^ other))
+        for xh in range(2) for zh in range(2) for zl in range(2) for c in range(2) for f in range(8)
+    )
 
 
 def swap(value, pairs):
@@ -388,51 +391,88 @@
                 grad_out[to : to + 16, lanes] = made[at : at + 16]
 
 
-def attend_back_body(
+def back_tiles(places, first, i, total, q_tiles, d_tiles, logs, deltas, keys, vals, keys_t, dk, dv):
+    q = [q_tiles[i * 2 + head] for head in range(2)]
+    grad = [d_tiles[i * 2 + head] for head in range(2)]
+    log = [logs[i * 2 + head : i * 2 + head + 1, :] for head in range(2)]
+    delta = [
+        jnp.concatenate([deltas[i * 2 + head, 0:1, :], deltas[i * 2 + head, 1:2, :]], axis=1)
+        for head in range(2)
+    ]
+    for lo, diagonal in places:
+        at = slice(lo, lo + 256)
+        here = slice(lo - first, lo - first + 256)
+        k, v = keys[at, :], vals[at, :]
+        dk_tile, dv_tile = dk[here, :], dv[here, :]
+        for head in range(2):
+            s = lax.dot_general(k, q[head], NT, preferred_element_type=F32)
+            p = jnp.exp2(s - log[head])
+            if diagonal:
+                row = lax.broadcasted_iota(jnp.int32, (256, 256), 0)
+                p = jnp.where(row <= lax.broadcasted_iota(jnp.int32, (256, 256), 1), p, 0.0)
+            dp = lax.dot_general(v, grad[head], NT, preferred_element_type=F32)
+            ds = (p * (dp - delta[head])).astype(BF16)
+            dv_tile += jnp.dot(p.astype(BF16), grad[head], preferred_element_type=F32)
+            dk_tile += jnp.dot(ds, q[head], preferred_element_type=F32)
+            total[head] = total[head] + jnp.dot(keys_t[:, here], ds, preferred_element_type=F32)
+        dk[here, :] = dk_tile
+        dv[here, :] = dv_tile
+    return total
+
+
+def low_back_body(
     ready, done, place, q_tiles, keys, vals, logs, d_tiles, deltas,
-    dq, dk, dv, d_low, dots, keys_t, dk_acc, dv_acc,
+    dq, d_low, dots, keys_t, dk_acc, dv_acc,
+):
+    ready(q_tiles, keys, vals, d_tiles)
+
+    @pl.when(place[0] == 1)
+    def _():
+        keys_t[...] = jnp.transpose(keys[:1024, :].astype(F32)).astype(BF16)
+        dk_acc[...] = jnp.zeros_like(dk_acc)
+        dv_acc[...] = jnp.zeros_like(dv_acc)
+        for i in range(4):
+            total = back_tiles(
+                [(lo, False) for lo in range(0, 1024, 256)], 0, i, [0.0, 0.0],
+                q_tiles, d_tiles, logs, deltas, keys, vals, keys_t, dk_acc, dv_acc,
+            )
+            for head in range(2):
+                dq[i * 2 + head] = total[head]
+        for b in range(8):
+            rows = slice(b * 128, b * 128 + 128)
+            key_grad = dk_acc[rows, :] * (1.0 / LOG2E)
+            d_low[rows, :128] = key_grad.astype(BF16)
+            d_low[rows, 128:] = dv_acc[rows, :].astype(BF16)
+            dots[b : b + 1, :] = row_sums(key_grad * keys[rows, :].astype(F32))
+
+    @pl.when(place[0] == 0)
+    def _():
+        dq[...] = jnp.zeros_like(dq)
+        d_low[...] = jnp.zeros_like(d_low)
+        dots[...] = jnp.zeros_like(dots)
+
+
+def own_back_body(
+    ready, done, place, q_tiles, keys, vals, logs, d_tiles, deltas, dq_low, dots_low,
+    dq, dk, dv, dots, keys_t, dk_acc, dv_acc,
 ):
     ready(keys)
-    keys_t[...] = jnp.transpose(keys[...].astype(F32)).astype(BF16)
-    ready(q_tiles, vals, d_tiles)
+    keys_t[...] = jnp.transpose(keys[1024:, :].astype(F32)).astype(BF16)
     dk_acc[...] = jnp.zeros_like(dk_acc)
     dv_acc[...] = jnp.zeros_like(dv_acc)
-    allowed = lax.broadcasted_iota(jnp.int32, (256, 256), 0) <= lax.broadcasted_iota(
-        jnp.int32, (256, 256), 1
-    )
-
-    def queries(first, i):
-        at_diagonal = 1024 + i * 256
-        q = [q_tiles[i * 2 + head] for head in range(2)]
-        grad = [d_tiles[i * 2 + head] for head in range(2)]
-        log = [logs[i * 2 + head : i * 2 + head + 1, :] for head in range(2)]
-        delta = [
-            jnp.concatenate([deltas[i * 2 + head, 0:1, :], deltas[i * 2 + head, 1:2, :]], axis=1)
-            for head in range(2)
-        ]
-        total = [0.0, 0.0]
-        for lo in range(first, at_diagonal + 256, 256):
-            at = slice(lo, lo + 256)
-            k, v = keys[at, :], vals[at, :]
-            dk_tile, dv_tile = dk_acc[at, :], dv_acc[at, :]
-            for head in range(2):
-                s = lax.dot_general(k, q[head], NT, preferred_element_type=F32)
-                p = jnp.exp2(s - log[head])
-                if lo == at_diagonal:
-                    p = jnp.where(allowed, p, 0.0)
-                dp = lax.dot_general(v, grad[head], NT, preferred_element_type=F32)
-                ds = (p * (dp - delta[head])).astype(BF16)
-                dv_tile += jnp.dot(p.astype(BF16), grad[head], preferred_element_type=F32)
-                dk_tile += jnp.dot(ds, q[head], preferred_element_type=F32)
-                total[head] = total[head] + jnp.dot(
-                    keys_t[:, at], ds, preferred_element_type=F32
-                )
-            dk_acc[at, :] = dk_tile
-            dv_acc[at, :] = dv_tile
+    ready(q_tiles, vals, d_tiles, dq_low)
+    for i in range(4):
+        total = back_tiles(
+            [(1024 + j * 256, j == i) for j in range(i + 1)], 1024, i,
+            [dq_low[i * 2 + head] for head in range(2)],
+            q_tiles, d_tiles, logs, deltas, keys, vals, keys_t, dk_acc, dv_acc,
+        )
         dot = jnp.zeros((1, 256), F32)
         for head in range(2):
             out = jnp.transpose(total[head]) * DH ** (-0.5)
-            dot += jnp.sum(total[head] * jnp.transpose(q[head].astype(F32)), axis=0, keepdims=True)
+            dot += jnp.sum(
+                total[head] * jnp.transpose(q_tiles[i * 2 + head].astype(F32)), axis=0, keepdims=True
+            )
             for c in range(2):
                 block = lax.rem(i - place[1] + 4, 4) + 4 * jnp.abs(c - place[2])
                 at = pl.ds(pl.multiple_of(block * 128, 128), 128)
@@ -440,29 +480,16 @@
         for c in range(2):
             block = lax.rem(i - place[1] + 4, 4) + 4 * jnp.abs(c - place[2])
             dots[pl.ds(block, 1), :] = dot[:, c * 128 : c * 128 + 128] * (1.0 / LOG2E)
-
-    @pl.when(place[0] == 1)
-    def _():
-        for i in range(4):
-            queries(0, i)
-
-    @pl.when(place[0] == 0)
-    def _():
-        for i in range(4):
-            queries(1024, i)
-
+    done(dq)
     for b in range(8):
         rows = slice(b * 128, b * 128 + 128)
         z, c = spot(place, b)
-        at = pl.ds(pl.multiple_of(1024 + z * 256 + c * 128, 128), 128)
-        key_grad = dk_acc[at, :] * (1.0 / LOG2E)
+        at = pl.multiple_of(z * 256 + c * 128, 128)
+        key_grad = dk_acc[pl.ds(at, 128), :] * (1.0 / LOG2E)
         dk[rows, :] = key_grad
-        dv[rows, :] = dv_acc[at, :]
-        dots[8 + b : 9 + b, :] = row_sums(key_grad * keys[at, :].astype(F32))
-        key_grad = dk_acc[rows, :] * (1.0 / LOG2E)
-        d_low[rows, :128] = key_grad.astype(BF16)
-        d_low[rows, 128:] = dv_acc[rows, :].astype(BF16)
-        dots[16 + b : 17 + b, :] = row_sums(key_grad * keys[rows, :].astype(F32))
+        dv[rows, :] = dv_acc[pl.ds(at, 128), :]
+        dots[8 + b : 9 + b, :] = row_sums(key_grad * keys[pl.ds(1024 + at, 128), :].astype(F32))
+    dots[16:24, :] = dots_low[...]
 
 
 def unproject_body(
@@ -536,17 +563,17 @@
     lax.fori_loop(0, 2, step, 0)
 
 
-def expand_body(ready, done, h_all, weight, gate, up, expanded, m_mine, m_part, down):
-    ready(weight)
+def expand_body(ready, done, h_all, weight, packed, gate, up, expanded, m_mine, m_part, down):
+    ready(packed)
     for f in range(8):
-        down[f * 96 : f * 96 + 96, :768] = weight[f * 128 : f * 128 + 96, 1536:]
+        down[f * 96 : f * 96 + 96, :768] = packed[f * 128 : f * 128 + 96, :]
         for m in range(3):
-            down[f * 96 + m * 32 : f * 96 + m * 32 + 32, 768:] = weight[
-                f * 128 + 96 : f * 128 + 128, 1536 + m * 256 : 1792 + m * 256
+            down[f * 96 + m * 32 : f * 96 + m * 32 + 32, 768:] = packed[
+                f * 128 + 96 : f * 128 + 128, m * 256 : m * 256 + 256
             ]
 
     done(down)
-    ready(h_all)
+    ready(h_all, weight)
     done(h_all)
 
     def widen(n, carry):
@@ -592,7 +619,7 @@
 
     def narrow(n, carry):
         lanes = pl.ds(pl.multiple_of(n * 256, 256), 256)
-        dh = lax.dot_general(d_gu[...], weight[lanes, :1536], NT, preferred_element_type=F32)
+        dh = lax.dot_general(d_gu[...], weight[lanes, :], NT, preferred_element_type=F32)
         dh_mine[:, lanes] = dh[:256]
         dh_part[:, lanes] = dh[256:].astype(BF16)
         return carry
@@ -708,8 +735,9 @@
         ],
         axis=0,
     )
-    w_mlp = jnp.concatenate([quarters(w_gate), quarters(w_up), packed], axis=1)
-    weight, w_mlp, w_out_rows = lax.optimization_barrier((weight, w_mlp, w_out_rows))
+    w_narrow = lax.all_gather(packed, "fsdp", axis=0, tiled=True)
+    w_wide = jnp.concatenate([quarters(w_gate), quarters(w_up)], axis=1)
+    weight, w_wide, w_out_rows = lax.optimization_barrier((weight, w_wide, w_out_rows))
 
     cosine, sine = rotary_tables(xh * 1024, z, c)
     gain_q = lax.dynamic_slice_in_dim(gain_query, zc * 256, 256, 0)[None]
@@ -728,10 +756,13 @@
     )
 
     kv_low = swap(kv_rot, LOW_TO_HIGH)
-    w_mlp = lax.all_gather(after(w_mlp, squares), "fsdp", axis=0, tiled=True)
     squares = sum_group(squares)
     squares_low = swap(squares[8:], LOW_TO_HIGH)
-    w_out_rows = spread(after(w_out_rows, squares_low))
+    kv_low, squares, squares_low, w_wide, w_narrow, w_out_rows = lax.optimization_barrier(
+        (kv_low, squares, squares_low, w_wide, w_narrow, w_out_rows)
+    )
+    w_wide = lax.all_gather(w_wide, "fsdp", axis=0, tiled=True)
+    w_out_rows = spread(w_out_rows)
     out_raw, mixed, mixed_turned, q_tiles, keys, vals, logs = kernel_call(
         attend_body,
         [
@@ -765,7 +796,7 @@
             shaped((256, 1024), F32), shaped((256, 1024), BF16), shaped((768, 1024), BF16),
         ],
         [
-            gather_pair(hidden_state.astype(BF16)), *in_hbm(w_mlp),
+            gather_pair(hidden_state.astype(BF16)), *in_hbm(w_wide, w_narrow),
         ],
         flops=2 * 512 * 2304 * 1024, nbytes=12 << 20,
     )
@@ -788,7 +819,7 @@
         [
             0, shaped((512, 1536), BF16), shaped((256, 1024), F32), shaped((256, 1024), BF16),
         ],
-        [d_blocks, gate, up, w_mlp, w_down_rows],
+        [d_blocks, gate, up, w_wide, w_down_rows],
         flops=2 * 512 * 2304 * 1024, nbytes=12 << 20,
     )
 
@@ -815,23 +846,8 @@
         [place, *in_hbm(out_raw, w_out_rows, gather_group(d_attended), mixed_turned)],
         flops=4 * 1024 * 1024 * 256, nbytes=6 << 20,
     )
-    dq, dk, dv, d_low, dots = kernel_call(
-        attend_back_body,
-        [
-            *in_hbm(
-                shaped((1024, 256), BF16), shaped((1024, 128), F32), shaped((1024, 128), F32),
-                shaped((1024, 256), BF16),
-            ),
-            shaped((24, 128), F32),
-        ],
-        [place, *in_hbm(q_tiles, keys, vals), logs, d_tiles, deltas],
-        [
-            pltpu.VMEM((128, 2048), BF16), pltpu.VMEM((2048, 128), F32),
-            pltpu.VMEM((2048, 128), F32),
-        ],
-        flops=10 * 1024 * 2048 * 256, nbytes=8 << 20,
-    )
     fsdp = lax.axis_index("fsdp")
+
     def halve(value, rows, bit, axis, pairs):
         parts = value.reshape(-1, 2, rows, 1024)
         given = jnp.where(bit == 1, parts[:, 0], parts[:, 1])
@@ -839,6 +855,35 @@
         return (mine + lax.ppermute(given, axis, pairs).astype(F32)).astype(BF16)
 
     grad_out = halve(grad_out, 32, fsdp % 2, "fsdp", [(i, i ^ 1) for i in range(8)])
+    scratch = [
+        pltpu.VMEM((128, 1024), BF16), pltpu.VMEM((1024, 128), F32), pltpu.VMEM((1024, 128), F32),
+    ]
+    shared = [place, *in_hbm(q_tiles, keys, vals), logs, d_tiles, deltas]
+    dq_low, d_low, dots_low = kernel_call(
+        low_back_body,
+        [
+            shaped((8, 128, 256), F32), *in_hbm(shaped((1024, 256), BF16)), shaped((8, 128), F32),
+        ],
+        shared,
+        scratch,
+        flops=10 * 1024 * 1024 * 256, nbytes=4 << 20,
+    )
+    dq_low, grad_out = lax.optimization_barrier((dq_low, grad_out))
+    grad_out = halve(grad_out, 32, fsdp // 2 % 2, "fsdp", [(i, i ^ 2) for i in range(8)])
+    dq, dk, dv, dots = kernel_call(
+        own_back_body,
+        [
+            *in_hbm(
+                shaped((1024, 256), BF16), shaped((1024, 128), F32), shaped((1024, 128), F32),
+            ),
+            shaped((24, 128), F32),
+        ],
+        [*shared, dq_low, dots_low],
+        scratch,
+        flops=10 * 1024 * 640 * 256, nbytes=5 << 20,
+    )
+    dots, grad_out = lax.optimization_barrier((dots, grad_out))
+    grad_out = halve(grad_out, 32, fsdp // 4, "fsdp", [(i, i ^ 4) for i in range(8)])
     d_got = swap(d_low, HIGH_TO_LOW)
     dots = sum_group(dots)
     dots_got = swap(dots[16:], HIGH_TO_LOW)
@@ -864,15 +909,14 @@
 
     mine, given = halves(grad_mlp, xh == 1)
     mine = mine.astype(F32) + swap(given, X_SWAP).astype(F32)
-    grad_out = after(grad_out, sent)
-    grad_out = halve(grad_out, 32, fsdp // 2 % 2, "fsdp", [(i, i ^ 2) for i in range(8)])
-    grad_out = halve(grad_out, 32, fsdp // 4, "fsdp", [(i, i ^ 4) for i in range(8)])
+    sent, grad_out = lax.optimization_barrier((sent, grad_out))
+    grad_out = halve(grad_out, 16, xh, "seq", X_SWAP)
     got_made = lax.all_to_all(
         sent.reshape(128, 8, 640), ("seq", "fsdp"), split_axis=0, concat_axis=0, tiled=True
     )
     dx_mine, dx_part = kernel_call(
         input_body,
-        [shaped((512, 1024), F32), shaped((512, 1024), BF16)],
+        in_hbm(shaped((512, 1024), F32), shaped((512, 1024), BF16)),
         [after(d_made, sent), weight],
         flops=2 * 1024 * 1024 * 512, nbytes=5 << 20,
     )
@@ -882,31 +926,34 @@
     d_inputs = pieces[0] + sum(
         swap(piece, to_z(k)).astype(F32) for k, piece in enumerate(far, 1)
     )
+    got_made, mine, grad_out, d_inputs = lax.optimization_barrier(
+        (got_made, mine, grad_out, d_inputs)
+    )
+    grad_out = swap(grad_out.reshape(16, 1024), OUT_HOME)
+    mine = mine.astype(BF16)
     grad_down = jnp.concatenate(
         [
-            mine[:48, 1536:2304],
+            mine[:48, 1536:],
             jnp.concatenate([mine[48:, 1536 + m * 256 : 1792 + m * 256] for m in range(3)], axis=0),
         ],
         axis=1,
     )
-    grad_down, given_down = halves(grad_down, z >= 2)
-    mine, given = halves(mine[:, :1536], z >= 2)
-    given = swap(
-        jnp.concatenate([given.reshape(48, 1024), given_down], axis=0).astype(BF16), FAR_SWAP
-    ).astype(F32)
-    mine = (mine + given[:48].reshape(32, 1536)).astype(BF16)
-    grad_down = (grad_down + given[48:]).astype(BF16)
-
-    got_made, mine, grad_down, grad_out, d_inputs = lax.optimization_barrier(
-        (got_made, mine, grad_down, grad_out, d_inputs)
-    )
-    grad_out = halve(grad_out, 16, xh, "seq", X_SWAP)
-    grad_out = swap(grad_out.reshape(16, 1024), OUT_HOME)
-    grad_down = lax.ppermute(grad_down, ("seq", "fsdp"), DOWN_HOME)
-    mine, given = halves(mine, z % 2 == 1)
-    got = swap(given, Z_SWAP)
-    mine = jnp.stack([jnp.where(z % 2 == 1, got, mine), jnp.where(z % 2 == 1, mine, got)])
-    mine = mine.reshape(2, 2, 8, 1536)
+    grad_down = sum(
+        lax.ppermute(
+            jnp.where((z >= 2) != other, grad_down[24:], grad_down[:24]),
+            ("seq", "fsdp"),
+            down_home(other),
+        ).astype(F32)
+        for other in (False, True)
+    )
+    mine = mine[:, :1536].reshape(4, 16, 1536)
+    terms = []
+    for k in range(4):
+        piece = lax.dynamic_index_in_dim(mine, (z + k) % 4, 0, keepdims=False)
+        terms.append(swap(piece, to_z(k)) if k else piece)
+    near = (terms[0].astype(F32) + terms[2].astype(F32)).astype(BF16).reshape(2, 8, 1536)
+    off = (terms[1].astype(F32) + terms[3].astype(F32)).astype(BF16).reshape(2, 8, 1536)
+    mine = jnp.stack([jnp.where(z % 2 == 1, off, near), jnp.where(z % 2 == 1, near, off)])
     given = jnp.where(c == 1, mine[:, 0], mine[:, 1])
     mine = jnp.where(c == 1, mine[:, 1], mine[:, 0])
     got = swap(given, CORE_SWAP)

time: 359 us -> 352 us (0.981)
  other arithmetic: 30.9 us -> 22.7 us
  local copies, waits for them, and re-layouts: 31.8 us -> 25.3 us
  Pallas kernels: 68.9 us -> 73 us
    ppermute x4, waiting for transfers between devices: 16.3 us -> 7.79 us  [halve(): return (mine + lax.ppermute(given, axis, pairs).astype(F32)).astype(BF16)]
    ppermute x1 -> x2, waiting for transfers between devices: 0.01 us -> 6.61 us  [on_device(): lax.ppermute(jnp.where((z >= 2) != other, grad_down[24:], grad_down[:24])...]
    ppermute x4, starting transfers between devices: 3.5 us -> 8.33 us  [halve(): return (mine + lax.ppermute(given, axis, pairs).astype(F32)).astype(BF16)]
    ppermute x55 -> x56, waiting for transfers between devices: 101 us -> 106 us  [swap(): return lax.ppermute(value, 'seq', pairs)]
    pallas_call x10 -> x11, Pallas kernels: 68.9 us -> 73 us  [kernel_call(): pl.pallas_call(whole, out_shape=tuple(shapes), in_specs=[where(s) for gro...]
    ppermute x55 -> x56, starting transfers between devices: 42.8 us -> 45.3 us  [swap(): return lax.ppermute(value, 'seq', pairs)]
    unnamed x65 -> x49, local copies, waits for them, and re-layouts: 7.53 us -> 5.16 us
  transfers between devices with their start and end apart: 66 -> 69, of which waited for: 31 -> 33; matrix products, arithmetic and copies ran while one was open for 16% -> 13% of each run, Pallas kernels for 15% -> 18%
where the time goes in v1:
time: 352 us; the launch traced here: 345 us
  waiting for transfers between devices  126 us (36%)
  starting transfers between devices  81.6 us (23%)
  Pallas kernels  73 us (21%)
  local copies, waits for them, and re-layouts  25.3 us (7%)
  other arithmetic  22.7 us (6%)
  between operations  14.9 us (4%)
    ppermute x56, waiting for transfers between devices, swap(): return lax.ppermute(value, 'seq', pairs)  106 us
    pallas_call x11, Pallas kernels, kernel_call(): pl.pallas_call(whole, out_shape=tuple(shapes), in_specs=[where(s) for gro...  73 us
    ppermute x56, starting transfers between devices, swap(): return lax.ppermute(value, 'seq', pairs)  45.3 us
    all_to_all x2, starting transfers between devices, spread(): lax.all_to_all(jnp.broadcast_to(block[None], (8,) + block.shape), 'fsdp',...  12.2 us
    ppermute x4, starting transfers between devices, halve(): return (mine + lax.ppermute(given, axis, pairs).astype(F32)).astype(BF16)  8.33 us
    ppermute x4, waiting for transfers between devices, halve(): return (mine + lax.ppermute(given, axis, pairs).astype(F32)).astype(BF16)  7.79 us
    all_to_all x1, starting transfers between devices, on_device(): lax.all_to_all(sent.reshape(128, 8, 640), ('seq', 'fsdp'), split_axis=0,...  7.57 us
  transfers between devices with their start and end apart: 69, of which 33 were waited for; matrix products, arithmetic and copies ran while one was open for 13% of the time, Pallas kernels for 18%

profile of v1, /device:TPU:6, one launch (start us, length us, event | category | flops | bytes accessed | tf_op | source)
XLA Modules:
  0.0 345.1 jit_solution(4823735998325492965)
XLA Ops:
  16.9 5.9 %all-to-all-start = ((bf16[8,128,512]{2,1,0:T(8,128)(2,1)}), bf16[8,128,512]{2,1,0:T(8,128)(2,1)S(1)}, u32[]{:S(2)}, u32[]{:S(2)}) async-start(bf16[8,128,512]{2,1,0:T(8,128)(2,1)} %broadcast_in_dim.14), calls=%async_computation | async-start | bytes 2097152 | tf_op jit(solution)/shard_map/all_to_all | solution.py:709
  42.9 5.7 %collective-permute-done.7 = bf16[32,1024]{1,0:T(8,128)(2,1)S(1)} collective-permute-done((bf16[32,1024]{1,0:T(8,128)(2,1)S(1)}, bf16[32,1024]{1,0:T(8,128)(2,1)S(1)}, u32[]{:S(2)}, u32[]{:S(2)}) %collective-permute-start.7) | collective-permute-done | bytes 65568 | tf_op jit(solution)/shard_map/ppermute | solution.py:720
  48.7 5.5 %shard_map.228 = (bf16[1024,1024]{1,0:T(8,128)(2,1)}, f32[1024,256]{1,0:T(8,128)}, f32[1024,128]{1,0:T(8,128)}, bf16[1024,256]{1,0:T(8,128)(2,1)}, bf16[1024,256]{1,0:T(8,128)(2,1)}, /*index=5*/f32[16,128]{1,0:T(8,128)S(1)}) custom-call(bf16[128,1024]{1,0:T(8,128)(2,1)S(1)} %bitcast.154, bf16[128,1024]{1,0:T(8,128)(2,1)S(1)} %collective-permute-done.refs_1_, ...), custom_call_target="tpu_custom_call" | custom-call | flops 1073741824 | bytes 9437184 | tf_op jit(solution)/shard_map/pallas_call | solution.py:220
  59.2 4.6 %collective-permute-start.11 = (f32[2,2,4,128]{3,2,1,0:T(4,128)S(1)}, f32[2,2,4,128]{3,2,1,0:T(4,128)S(1)}, u32[]{:S(2)}, u32[]{:S(2)}) collective-permute-start(f32[2,2,4,128]{3,2,1,0:T(4,128)S(1)} %get-tuple-element.162), channel_id=1, source_target_pairs={{0,32},{8,40},{16,48},{24,56},{32,0},{40,8},{48,16},{56,24},{64,96... | collective-permute-start | bytes 24584 | tf_op jit(solution)/shard_map/ppermute | solution.py:67
  66.8 14.1 %collective-permute-done.12.refs_5_ = f32[8,128]{1,0:T(8,128)S(1)} collective-permute-done((f32[8,128]{1,0:T(8,128)S(1)}, f32[8,128]{1,0:T(8,128)S(1)}, u32[]{:S(2)}, u32[]{:S(2)}) %collective-permute-start.12) | collective-permute-done | bytes 4128 | tf_op jit(solution)/shard_map/ppermute | solution.py:67
  81.9 6.2 %all-to-all-start.1 = ((bf16[8,32,1024]{2,1,0:T(8,128)(2,1)}), bf16[8,32,1024]{2,1,0:T(8,128)(2,1)S(1)}, u32[]{:S(2)}, u32[]{:S(2)}) async-start(bf16[8,32,1024]{2,1,0:T(8,128)(2,1)} %broadcast_in_dim.17), calls=%async_computation.1 | async-start | bytes 1048576 | tf_op jit(solution)/shard_map/all_to_all | solution.py:709
  88.2 12.1 %shard_map.229 = (f32[1024,256]{1,0:T(8,128)}, bf16[1024,256]{1,0:T(8,128)(2,1)}, bf16[256,1024]{1,0:T(8,128)(2,1)}, bf16[8,256,128]{2,1,0:T(8,128)(2,1)}, bf16[...) custom-call(s32[3]{0:T(128)S(1)} %pad_add_fusion.refs_0_, ...), custom_call_target="tpu_custom_call" | custom-call | flops 2147483648 | bytes 9437184 | tf_op jit(solution)/shard_map/pallas_call | solution.py:220
  124.9 8.0 %collective-permute-done.20.refs_1_ = bf16[128,1024]{1,0:T(8,128)(2,1)S(1)} collective-permute-done((bf16[128,1024]{1,0:T(8,128)(2,1)S(1)}, bf16[128,1024]{1,0:T(8,128)(2,1)S(1)}, u32[]{:S(2)}, u32[]{:S(2)}) %collective-permute-start.20) | collective-permute-done | bytes 262176 | tf_op jit(solution)/shard_map/ppermute | solution.py:67
  134.4 7.0 %shard_map.231 = (bf16[512,1024]{1,0:T(8,128)(2,1)S(1)}, f32[512,768]{1,0:T(8,128)S(1)}, f32[512,768]{1,0:T(8,128)S(1)}, bf16[512,768]{1,0:T(8,128)(2,1)S(1)}, f...) custom-call(bf16[128,1024]{1,0:T(8,128)(2,1)S(1)} %fusion.12.refs_0_, ...), custom_call_target="tpu_custom_call" | custom-call | flops 2415919104 | bytes 12582912 | tf_op jit(solution)/shard_map/pallas_call | solution.py:220
  143.5 8.1 %collective-permute-done.25 = bf16[128,1024]{1,0:T(8,128)(2,1)S(1)} collective-permute-done((bf16[128,1024]{1,0:T(8,128)(2,1)S(1)}, bf16[128,1024]{1,0:T(8,128)(2,1)S(1)}, u32[]{:S(2)}, u32[]{:S(2)}) %collective-permute-start.25) | collective-permute-done | bytes 262176 | tf_op jit(solution)/shard_map/ppermute | solution.py:67
  152.6 7.2 %collective-permute-done.26.refs_1_ = bf16[128,1024]{1,0:T(8,128)(2,1)S(1)} collective-permute-done((bf16[128,1024]{1,0:T(8,128)(2,1)S(1)}, bf16[128,1024]{1,0:T(8,128)(2,1)S(1)}, u32[]{:S(2)}, u32[]{:S(2)}) %collective-permute-start.26) | collective-permute-done | bytes 262176 | tf_op jit(solution)/shard_map/ppermute | solution.py:67
  161.7 5.1 %shard_map.232 = (bf16[512,1024]{1,0:T(8,128)(2,1)S(1)}, bf16[512,1536]{1,0:T(8,128)(2,1)S(1)}, f32[256,1024]{1,0:T(8,128)S(1)}, bf16[256,1024]{1,0:T(8,128)(2,1)S(1)}) custom-call(bf16[128,1024]{1,0:T(8,128)(2,1)S(1)} %fusion.7.refs_0_, bf16[128,1024]{1,0:T(8,128)(2,1)S(1)} %collective-permute-done.26.refs_1_, ...), custom_call_target="tpu_custom_call" | custom-call | flops 2415919104 | bytes 12582912 | tf_op jit(solution)/shard_map/pallas_call | solution.py:220
  170.3 6.4 %shard_map.233 = bf16[1024,2304]{1,0:T(8,128)(2,1)} custom-call(bf16[1024,512]{1,0:T(8,128)(2,1)S(1)} %fusion.2.refs_0_, bf16[512,1536]{1,0:T(8,128)(2,1)S(1)} %get-tuple-element.114.refs_1_, bf16[512,768]{1,0:T(8,128)(2,1)S(1)} %get-tuple-element.115.refs_2_, bf16[512,1024]{1,0:T(8,128)(2,1)S(1)} %get-tuple-element.116.refs_3_), custom_call_target="tpu_custom_call" | custom-call | flops 2415919104 | bytes 9437184 | tf_op jit(solution)/shard_map/pallas_call | solution.py:220
  185.7 6.8 %collective-permute-done.32.refs_4_ = bf16[128,1024]{1,0:T(8,128)(2,1)S(1)} collective-permute-done((bf16[128,1024]{1,0:T(8,128)(2,1)S(1)}, bf16[128,1024]{1,0:T(8,128)(2,1)S(1)}, u32[]{:S(2)}, u32[]{:S(2)}) %collective-permute-start.32) | collective-permute-done | bytes 262176 | tf_op jit(solution)/shard_map/ppermute | solution.py:67
  201.3 5.1 %shard_map.234 = (bf16[8,256,128]{2,1,0:T(8,128)(2,1)S(1)}, f32[8,2,128]{2,1,0:T(2,128)S(1)}, bf16[256,1024]{1,0:T(8,128)(2,1)S(1)}) custom-call(s32[3]{0:T(128)S(1)} %pad_add_fusion.refs_0_, f32[1024,256]{1,0:T(8,128)} %get-tuple-element.122.refs_1_, bf16[256,1024]{1,0:T(8,128)(2,1)} %bitcast.156, bf16[128,1024]{1,0:T(8,128)(2,1)} %copy-done.14, ...), custom_call_target="tpu_custom_call" | custom-call | flops 1073741824 | bytes 6291456 | tf_op jit(solution)/shard_map/pallas_call | solution.py:220
  208.8 10.6 %shard_map.235 = (f32[8,128,256]{2,1,0:T(8,128)S(1)}, bf16[1024,256]{1,0:T(8,128)(2,1)}, f32[8,128]{1,0:T(8,128)S(1)}) custom-call(s32[3]{0:T(128)S(1)} %pad_add_fusion.refs_0_, bf16[8,256,128]{2,1,0:T(8,128)(2,1)} %get-tuple-element.118.refs_1_, bf16[2048,128]{1,0:T(8,128)(2,1)} %get-tuple-element.119.refs_2_, ...), custom_call_target="tpu_custom_call" | custom-call | flops 2684354560 | bytes 4194304 | tf_op jit(solution)/shard_map/pallas_call | solution.py:220
  226.5 8.2 %shard_map.236 = (bf16[1024,256]{1,0:T(8,128)(2,1)}, f32[1024,128]{1,0:T(8,128)}, f32[1024,128]{1,0:T(8,128)}, f32[24,128]{1,0:T(8,128)S(1)}) custom-call(s32[3]{0:T(128)S(1)} %pad_add_fusion.refs_0_, bf16[8,256,128]{2,1,0:T(8,128)(2,1)} %get-tuple-element.118.refs_1_, bf16[2048,128]{1,0:T(8,128)(2,1)} %get-tuple-element.119.refs_2_, ...), custom_call_target="tpu_custom_call" | custom-call | flops 1677721600 | bytes 5242880 | tf_op jit(solution)/shard_map/pallas_call | solution.py:220
  246.5 5.2 %collective-permute-done.46 = bf16[1,32,1024]{2,1,0:T(8,128)(2,1)S(1)} collective-permute-done((bf16[1,32,1024]{2,1,0:T(8,128)(2,1)S(1)}, bf16[1,32,1024]{2,1,0:T(8,128)(2,1)S(1)}, u32[]{:S(2)}, u32[]{:S(2)}) %collective-permute-start.46) | collective-permute-done | bytes 65568 | tf_op jit(solution)/shard_map/ppermute | solution.py:855
  251.7 7.3 %shard_map.237 = (bf16[1024,512]{1,0:T(8,128)(2,1)S(1)}, bf16[1024,640]{1,0:T(8,128)(2,1)}) custom-call(s32[3]{0:T(128)S(1)} %pad_add_fusion.refs_0_, bf16[1024,256]{1,0:T(8,128)(2,1)} %get-tuple-element.130.refs_1_, f32[1024,128]{1,0:T(8,128)} %get-tuple-element.131.refs_2_, f32[1024,128]{1,0:T(8,128)} %get-tuple-element.132.refs_3_, ...), custom_call_target="tpu_custom_call" | custom-call | flops 1073741824 | bytes 9437184 | tf_op jit(solution)/shard_map/pallas_call | solution.py:220
  267.8 7.6 %all-to-all-start.2 = ((bf16[128,8,640]{2,1,0:T(8,128)(2,1)}), bf16[128,8,640]{2,1,0:T(8,128)(2,1)S(1)}, u32[]{:S(2)}, u32[]{:S(2)}) async-start(bf16[128,8,640]{2,1,0:T(8,128)(2,1)} %bitcast.42), calls=%async_computation.2 | async-start | bytes 2621440 | tf_op jit(solution)/shard_map/all_to_all | solution.py:914
  286.0 13.8 %collective-permute-done.51 = bf16[128,1024]{1,0:T(8,128)(2,1)S(1)} collective-permute-done((bf16[128,1024]{1,0:T(8,128)(2,1)S(1)}, bf16[128,1024]{1,0:T(8,128)(2,1)S(1)}, u32[]{:S(2)}, u32[]{:S(2)}) %collective-permute-start.51) | collective-permute-done | bytes 262176 | tf_op jit(solution)/shard_map/ppermute | solution.py:67
  299.8 5.7 %collective-permute-done.53 = bf16[128,1024]{1,0:T(8,128)(2,1)} collective-permute-done((bf16[128,1024]{1,0:T(8,128)(2,1)S(1)}, bf16[128,1024]{1,0:T(8,128)(2,1)}, u32[]{:S(2)}, u32[]{:S(2)}) %collective-permute-start.53) | collective-permute-done | bytes 262176 | tf_op jit(solution)/shard_map/ppermute | solution.py:67
  321.5 6.8 %collective-permute-done.56 = bf16[16,1024]{1,0:T(8,128)(2,1)S(1)} collective-permute-done((bf16[16,1024]{1,0:T(8,128)(2,1)S(1)}, bf16[16,1024]{1,0:T(8,128)(2,1)S(1)}, u32[]{:S(2)}, u32[]{:S(2)}) %collective-permute-start.56) | collective-permute-done | bytes 32800 | tf_op jit(solution)/shard_map/ppermute | solution.py:67
  329.2 6.6 %collective-permute-done.62 = bf16[24,1024]{1,0:T(8,128)(2,1)S(1)} collective-permute-done((bf16[24,1024]{1,0:T(8,128)(2,1)S(1)}, bf16[24,1024]{1,0:T(8,128)(2,1)S(1)}, u32[]{:S(2)}, u32[]{:S(2)}) %collective-permute-start.62) | collective-permute-done | bytes 49184 | tf_op jit(solution)/shard_map/ppermute | solution.py:942
  (283 shorter events, 150.6 us)
Async XLA Ops:
  7.2 73.8 %all-gather.3.cloned.1.call-start = ((), (), s32[]{:S(2)}) async-start(), calls=%async_computation.4 | async-start | bytes 1769472 | tf_op jit(solution)/shard_map/all_gather | solution.py:738
  7.2 27.5 %collective-permute-start = (bf16[128,1024]{1,0:T(8,128)(2,1)}, bf16[128,1024]{1,0:T(8,128)(2,1)S(1)}, u32[]{:S(2)}, u32[]{:S(2)}) collective-permute-start(bf16[128,1024]{1,0:T(8,128)(2,1)} %bitcast.150), channel_id=1, source_target_pairs={{16,0},{24,8},{32,16},{40,24},{48,32},{56,40},{0,48},{8,56},{80,64... | collective-permute-start | bytes 786440 | tf_op jit(solution)/shard_map/ppermute | solution.py:67
  11.3 23.4 %collective-permute-start.1 = (bf16[128,1024]{1,0:T(8,128)(2,1)}, bf16[128,1024]{1,0:T(8,128)(2,1)S(1)}, u32[]{:S(2)}, u32[]{:S(2)}) collective-permute-start(bf16[128,1024]{1,0:T(8,128)(2,1)} %bitcast.151), channel_id=1, source_target_pairs={{32,0},{40,8},{48,16},{56,24},{0,32},{8,40},{16,48},{24,56},{96,64... | collective-permute-start | bytes 786440 | tf_op jit(solution)/shard_map/ppermute | solution.py:67
  11.4 23.9 %collective-permute-start.2 = (bf16[128,1024]{1,0:T(8,128)(2,1)}, bf16[128,1024]{1,0:T(8,128)(2,1)S(1)}, u32[]{:S(2)}, u32[]{:S(2)}) collective-permute-start(bf16[128,1024]{1,0:T(8,128)(2,1)} %bitcast.152), channel_id=1, source_target_pairs={{48,0},{56,8},{0,16},{8,24},{16,32},{24,40},{32,48},{40,56},{112,6... | collective-permute-start | bytes 786440 | tf_op jit(solution)/shard_map/ppermute | solution.py:67
  12.6 36.0 %collective-permute-start.3 = (bf16[128,1024]{1,0:T(8,128)(2,1)}, bf16[128,1024]{1,0:T(8,128)(2,1)S(1)}, u32[]{:S(2)}, u32[]{:S(2)}) collective-permute-start(bf16[128,1024]{1,0:T(8,128)(2,1)} %bitcast.153), channel_id=1, source_target_pairs={{0,8},{8,0},{16,24},{24,16},{32,40},{40,32},{48,56},{56,48},{64,72... | collective-permute-start | bytes 786440 | tf_op jit(solution)/shard_map/ppermute | solution.py:67
  16.9 31.7 %all-to-all-start = ((bf16[8,128,512]{2,1,0:T(8,128)(2,1)}), bf16[8,128,512]{2,1,0:T(8,128)(2,1)S(1)}, u32[]{:S(2)}, u32[]{:S(2)}) async-start(bf16[8,128,512]{2,1,0:T(8,128)(2,1)} %broadcast_in_dim.14), calls=%async_computation | async-start | bytes 2097152 | tf_op jit(solution)/shard_map/all_to_all | solution.py:709
  22.9 111.6 %all-gather.5.cloned.1.call-start = ((), (), s32[]{:S(2)}) async-start(), calls=%async_computation.5 | async-start | bytes 3538944 | tf_op jit(solution)/shard_map/all_gather | solution.py:764
  63.8 17.1 %collective-permute-start.8 = (bf16[1024,256]{1,0:T(8,128)(2,1)}, bf16[1024,256]{1,0:T(8,128)(2,1)S(1)}, u32[]{:S(2)}, u32[]{:S(2)}) collective-permute-start(bf16[1024,256]{1,0:T(8,128)(2,1)} %get-tuple-element.86.refs_2_), channel_id=1, source_target_pairs={{0,64},{8,72},{16,80},{24,88},{32,96},{40,104},{48,112},{56,120},{... | collective-permute-start | bytes 1572872 | tf_op jit(solution)/shard_map/ppermute | solution.py:67
  65.5 15.5 %collective-permute-start.12 = (f32[8,128]{1,0:T(8,128)S(1)}, f32[8,128]{1,0:T(8,128)S(1)}, u32[]{:S(2)}, u32[]{:S(2)}) collective-permute-start(f32[8,128]{1,0:T(8,128)S(1)} %bitcast.190), channel_id=1, source_target_pairs={{0,64},{8,72},{16,80},{24,88},{32,96},{40,104},{48,112},{56,120},{... | collective-permute-start | bytes 12296 | tf_op jit(solution)/shard_map/ppermute | solution.py:67
  81.9 18.7 %all-to-all-start.1 = ((bf16[8,32,1024]{2,1,0:T(8,128)(2,1)}), bf16[8,32,1024]{2,1,0:T(8,128)(2,1)S(1)}, u32[]{:S(2)}, u32[]{:S(2)}) async-start(bf16[8,32,1024]{2,1,0:T(8,128)(2,1)} %broadcast_in_dim.17), calls=%async_computation.1 | async-start | bytes 1048576 | tf_op jit(solution)/shard_map/all_to_all | solution.py:709
  88.1 195.0 %reduce-scatter.2.cloned.1.call-start = ((), (), s32[]{:S(2)}) async-start(), calls=%async_computation.6 | async-start | bytes 5308416 | tf_op jit(solution)/shard_map/reduce_scatter | solution.py:837
  107.7 15.3 %collective-permute-start.16 = (bf16[128,1024]{1,0:T(8,128)(2,1)}, bf16[128,1024]{1,0:T(8,128)(2,1)S(1)}, u32[]{:S(2)}, u32[]{:S(2)}) collective-permute-start(bf16[128,1024]{1,0:T(8,128)(2,1)} %get-tuple-element.169), channel_id=1, source_target_pairs={{0,16},{8,24},{16,32},{24,40},{32,48},{40,56},{48,0},{56,8},{64,80... | collective-permute-start | bytes 786440 | tf_op jit(solution)/shard_map/ppermute | solution.py:67
  207.2 14.9 %collective-permute-start.39 = (bf16[4,32,1024]{2,1,0:T(8,128)(2,1)}, bf16[4,32,1024]{2,1,0:T(8,128)(2,1)}, u32[]{:S(2)}, u32[]{:S(2)}) collective-permute-start(bf16[4,32,1024]{2,1,0:T(8,128)(2,1)} %fusion.13), channel_id=1, source_target_pairs={{0,1},{1,0},{2,3},{3,2},{4,5},{5,4},{6,7},{7,6},{8,9},{9,8},{10,11... | collective-permute-start | bytes 786440 | tf_op jit(solution)/shard_map/ppermute | solution.py:855
  236.2 15.5 %collective-permute-start.40 = (bf16[1024,256]{1,0:T(8,128)(2,1)S(1)}, bf16[1024,256]{1,0:T(8,128)(2,1)S(1)}, u32[]{:S(2)}, u32[]{:S(2)}) collective-permute-start(bf16[1024,256]{1,0:T(8,128)(2,1)S(1)} %copy-done.22), channel_id=1, source_target_pairs={{64,0},{72,8},{80,16},{88,24},{96,32},{104,40},{112,48},{120,56},{... | collective-permute-start | bytes 1572872 | tf_op jit(solution)/shard_map/ppermute | solution.py:67
  264.4 21.6 %collective-permute-start.49 = (bf16[128,1024]{1,0:T(8,128)(2,1)S(1)}, bf16[128,1024]{1,0:T(8,128)(2,1)}, u32[]{:S(2)}, u32[]{:S(2)}) collective-permute-start(bf16[128,1024]{1,0:T(8,128)(2,1)S(1)} %get-tuple-element.170), channel_id=1, source_target_pairs={{0,8},{8,0},{16,24},{24,16},{32,40},{40,32},{48,56},{56,48},{64,72... | collective-permute-start | bytes 786440 | tf_op jit(solution)/shard_map/ppermute | solution.py:67
  264.8 19.5 %collective-permute-start.48 = (bf16[1,16,1024]{2,1,0:T(8,128)(2,1)S(1)}, bf16[1,16,1024]{2,1,0:T(8,128)(2,1)S(1)}, u32[]{:S(2)}, u32[]{:S(2)}) collective-permute-start(bf16[1,16,1024]{2,1,0:T(8,128)(2,1)S(1)} %select_bitcast_fusion.5), channel_id=1, source_target_pairs={{0,64},{8,72},{16,80},{24,88},{32,96},{40,104},{48,112},{56,120},{... | collective-permute-start | bytes 98312 | tf_op jit(solution)/shard_map/ppermute | solution.py:855
  267.8 39.3 %all-to-all-start.2 = ((bf16[128,8,640]{2,1,0:T(8,128)(2,1)}), bf16[128,8,640]{2,1,0:T(8,128)(2,1)S(1)}, u32[]{:S(2)}, u32[]{:S(2)}) async-start(bf16[128,8,640]{2,1,0:T(8,128)(2,1)} %bitcast.42), calls=%async_computation.2 | async-start | bytes 2621440 | tf_op jit(solution)/shard_map/all_to_all | solution.py:914
  277.0 22.8 %collective-permute-start.51 = (bf16[128,1024]{1,0:T(8,128)(2,1)S(1)}, bf16[128,1024]{1,0:T(8,128)(2,1)S(1)}, u32[]{:S(2)}, u32[]{:S(2)}) collective-permute-start(bf16[128,1024]{1,0:T(8,128)(2,1)S(1)} %get-tuple-element.164), channel_id=1, source_target_pairs={{0,16},{8,24},{16,32},{24,40},{32,48},{40,56},{48,0},{56,8},{64,80... | collective-permute-start | bytes 786440 | tf_op jit(solution)/shard_map/ppermute | solution.py:67
  278.7 26.8 %collective-permute-start.53 = (bf16[128,1024]{1,0:T(8,128)(2,1)S(1)}, bf16[128,1024]{1,0:T(8,128)(2,1)}, u32[]{:S(2)}, u32[]{:S(2)}) collective-permute-start(bf16[128,1024]{1,0:T(8,128)(2,1)S(1)} %get-tuple-element.166), channel_id=1, source_target_pairs={{0,32},{8,40},{16,48},{24,56},{32,0},{40,8},{48,16},{56,24},{64,96... | collective-permute-start | bytes 786440 | tf_op jit(solution)/shard_map/ppermute | solution.py:67
  281.9 23.6 %collective-permute-start.55 = (bf16[128,1024]{1,0:T(8,128)(2,1)S(1)}, bf16[128,1024]{1,0:T(8,128)(2,1)}, u32[]{:S(2)}, u32[]{:S(2)}) collective-permute-start(bf16[128,1024]{1,0:T(8,128)(2,1)S(1)} %get-tuple-element.165), channel_id=1, source_target_pairs={{0,48},{8,56},{16,0},{24,8},{32,16},{40,24},{48,32},{56,40},{64,11... | collective-permute-start | bytes 786440 | tf_op jit(solution)/shard_map/ppermute | solution.py:67
  284.3 22.7 %collective-permute-start.47 = (bf16[64,2304]{1,0:T(8,128)(2,1)S(1)}, bf16[64,2304]{1,0:T(8,128)(2,1)S(1)}, u32[]{:S(2)}, u32[]{:S(2)}) collective-permute-start(bf16[64,2304]{1,0:T(8,128)(2,1)S(1)} %broadcast_select_fusion), channel_id=1, source_target_pairs={{0,64},{8,72},{16,80},{24,88},{32,96},{40,104},{48,112},{56,120},{... | collective-permute-start | bytes 884744 | tf_op jit(solution)/shard_map/ppermute | solution.py:67
  308.7 20.5 %collective-permute-start.61 = (bf16[24,1024]{1,0:T(8,128)(2,1)S(1)}, bf16[24,1024]{1,0:T(8,128)(2,1)S(1)}, u32[]{:S(2)}, u32[]{:S(2)}) collective-permute-start(bf16[24,1024]{1,0:T(8,128)(2,1)S(1)} %get-tuple-element.201), channel_id=1, source_target_pairs={{0,0},{1,16},{2,32},{3,48},{4,64},{5,80},{6,96},{7,112},{8,4},{9,2... | collective-permute-start | bytes 147464 | tf_op jit(solution)/shard_map/ppermute | solution.py:942
  313.1 15.9 %collective-permute-start.57 = (bf16[16,1536]{1,0:T(8,128)(2,1)S(1)}, bf16[16,1536]{1,0:T(8,128)(2,1)S(1)}, u32[]{:S(2)}, u32[]{:S(2)}) collective-permute-start(bf16[16,1536]{1,0:T(8,128)(2,1)S(1)} %get-tuple-element.196), channel_id=1, source_target_pairs={{0,16},{8,24},{16,32},{24,40},{32,48},{40,56},{48,0},{56,8},{64,80... | collective-permute-start | bytes 147464 | tf_op jit(solution)/shard_map/ppermute | solution.py:67
  314.2 14.8 %collective-permute-start.58 = (bf16[16,1536]{1,0:T(8,128)(2,1)S(1)}, bf16[16,1536]{1,0:T(8,128)(2,1)S(1)}, u32[]{:S(2)}, u32[]{:S(2)}) collective-permute-start(bf16[16,1536]{1,0:T(8,128)(2,1)S(1)} %get-tuple-element.195), channel_id=1, source_target_pairs={{0,48},{8,56},{16,0},{24,8},{32,16},{40,24},{48,32},{56,40},{64,11... | collective-permute-start | bytes 147464 | tf_op jit(solution)/shard_map/ppermute | solution.py:67
  (68 other events, 561.1 us)
Sparse Core Ops, SparseCore 0:
  15.1 47.4 all-gather.2
  81.1 44.8 all-gather.4
  179.1 62.8 reduce-scatter.1
